TPU v7x, 128 devices: a whole 4x4x4 slice. The times are simulated.
128 devices in a mesh: group: 8 (over x, core), block: 16 (over z, y).
Axes of the slice: x: 4, y: 4, z: 4, core: 2. Of those that a mesh axis runs over, the one named last changes fastest.
Arguments:
- embeddings: bfloat16 [131072, 1024], P(('group', 'block'))
- target: int32 [131072], P(('group', 'block')), may hold values from 0 to 131071, as said below
- cluster_labels: int32 [131072], P('group'), may hold values from 0 to 65535, as said below
Outputs:
- best_cosine: float32 [131072], P(('group', 'block'))
Inputs may be any that keep to these rules, and one draw needn't show every extreme that they name: target is a permutation. Number the devices group-major as d = group index * 16 + block index and let document i be the j-th of device d; then target[i] // 1024 runs over every device exactly 8 times among device d's documents, and target[i] % 1024 // 8 == d. `cluster_labels`: within each cluster group's 16384 rows the labels never fall; the labels of group g lie in [g * 8192, (g + 1) * 8192); every cluster is a contiguous run of 2 to 2048 rows inside one group, and each group has a cluster of exactly 2048 rows; different groups share no label.
All inputs are finite; a program needn't handle non-finite values.
Results may differ from a plain program's by a relative error of at most 0.00076.
Values may be sent and summed in bfloat16 or wider, within the bound.
A program may use at most 64 MiB of HBM per device.

v0:
```python
import jax
import jax.numpy as jnp
from jax import lax
from jax.sharding import PartitionSpec as P


def passed_along(x, axis, by):
    length = lax.axis_size(axis)
    pairs = [(i, i + by) for i in range(length) if 0 <= i + by < length]
    return lax.ppermute(x, axis, pairs)


def body(embeddings, target, cluster_labels):
    rows = embeddings.shape[0]
    groups = lax.axis_size("group")
    blocks = lax.axis_size("block")
    slot = rows // (groups * blocks)
    block_id = lax.axis_index("block")
    values = embeddings.astype(jnp.float32)
    squares = jnp.sum(values * values, axis=1, keepdims=True)
    unit = (values * lax.rsqrt(squares + 1e-06)).astype(jnp.bfloat16)
    position = target // rows * slot + target % slot
    outgoing = jnp.zeros_like(unit).at[position].set(unit)
    received = lax.all_to_all(outgoing, ("group", "block"), split_axis=0, concat_axis=0, tiled=True)
    own_start = block_id * rows
    own_labels = lax.dynamic_slice_in_dim(cluster_labels, own_start, rows, 0)
    own_rows = own_start + jnp.arange(rows, dtype=jnp.int32)

    def masked_gram(piece, start):
        count = piece.shape[0]
        piece_labels = lax.dynamic_slice_in_dim(cluster_labels, start, count, 0)
        gram = lax.dot_general(
            received, piece, (((1,), (1,)), ((), ())), preferred_element_type=jnp.float32
        )
        piece_rows = start + jnp.arange(count, dtype=jnp.int32)
        same = (own_labels[:, None] == piece_labels[None, :]) & (
            own_rows[:, None] != piece_rows[None, :]
        )
        return jnp.where(same, gram, jnp.float32(-2.0))

    def correlations(piece, start):
        count = piece.shape[0]
        piece_labels = lax.dynamic_slice_in_dim(cluster_labels, start, count, 0)
        return (piece_labels[0] <= own_labels[-1]) & (piece_labels[-1] >= own_labels[0])

    def add_tile(best, piece, start, valid):
        needed = valid & correlations(piece, start)

        def compute(current):
            return jnp.maximum(current, jnp.max(masked_gram(piece, start), axis=1))

        return lax.cond(needed, compute, lambda current: current, best)

    initial = jnp.full((rows,), -2.0, jnp.float32)
    row_best = add_tile(initial, received, own_start, jnp.bool_(True))
    for offset in (1, -1, 2, -2):
        other = passed_along(received, "block", offset)
        source = block_id - offset
        valid = (source >= 0) & (source < blocks)
        start = jnp.clip(source, 0, blocks - 1) * rows
        row_best = add_tile(row_best, other, start, valid)
    returned = lax.all_to_all(row_best, ("group", "block"), split_axis=0, concat_axis=0, tiled=True)
    return returned[position]


def solution(mesh):
    return jax.shard_map(
        body,
        mesh=mesh,
        in_specs=(P(("group", "block"), None), P(("group", "block")), P("group")),
        out_specs=P(("group", "block")),
        check_vma=False,
    )
```

profile of v0, /device:TPU:1, one launch (start us, length us, event | category | flops | bytes accessed | tf_op | source)
XLA Modules:
  0.0 231.6 jit_solution(2426847682603731620)
XLA Ops:
  0.0 0.8 broadcast_clamp_fusion
  0.9 2.1 fusion
  2.9 7.2 %scatter_custom_fusion = bf16[1024,1024]{1,0:T(8,128)(2,1)} fusion(s32[1024]{0:T(1024)S(1)} %get-tuple-element.124, bf16[1024,1024]{1,0:T(8,128)(2,1)S(1)} %copy-done, f32[1024]{0:T(1024)S(1)} %add_rsqrt_fusion, bf16[]{:T(256)} %constant.97.clone.1), kind=kCustom, calls=%fused_computation.17 | custom fusion | flops 3145728 | bytes 4198402 | tf_op jit(solution)/shard_map/scatter | solution.py:23
  10.2 40.8 %all_to_all.24 = bf16[128,8,1024]{2,1,0:T(8,128)(2,1)S(1)} all-to-all(bf16[128,8,1024]{2,1,0:T(8,128)(2,1)} %bitcast.19), channel_id=1, replica_groups=mesh['group'=8,'block'=16] {'group','block'}, dimensions={0} | all-to-all | bytes 4194304 | tf_op jit(solution)/shard_map/all_to_all | solution.py:24
  51.0 4.4 %collective-permute-start = (bf16[1024,1024]{1,0:T(8,128)(2,1)S(1)}, bf16[1024,1024]{1,0:T(8,128)(2,1)}, u32[]{:S(2)}, u32[]{:S(2)}) collective-permute-start(bf16[1024,1024]{1,0:T(8,128)(2,1)S(1)} %bitcast.20), channel_id=1, source_target_pairs={{0,1},{1,2},{2,3},{3,4},{4,5},{5,6},{6,7},{7,8},{8,9},{9,10},{10,1... | collective-permute-start | bytes 6291464 | tf_op jit(solution)/shard_map/ppermute | solution.py:10
  55.3 1.3 collective-permute-start.1
  56.6 5.0 %collective-permute-start.2 = (bf16[1024,1024]{1,0:T(8,128)(2,1)S(1)}, bf16[1024,1024]{1,0:T(8,128)(2,1)}, u32[]{:S(2)}, u32[]{:S(2)}) collective-permute-start(bf16[1024,1024]{1,0:T(8,128)(2,1)S(1)} %bitcast.22), channel_id=1, source_target_pairs={{0,2},{1,3},{2,4},{3,5},{4,6},{5,7},{6,8},{7,9},{8,10},{9,11},{10,... | collective-permute-start | bytes 6291464 | tf_op jit(solution)/shard_map/ppermute | solution.py:10
  61.6 1.3 collective-permute-start.3
  62.9 0.7 fusion.14
  66.1 0.6 fusion.16
  71.7 0.6 fusion.12
  77.5 2.9 %conditional.5 = (f32[1024]{0:T(1024)S(1)}) conditional(s32[]{:T(128)} %bitcast.4, () %tuple.35, (s32[1024]{0:T(1024)S(1)}, s32[]{:T(128)}, s32[16384]{0:T(1024)S(1)}, s32[1024]{0:T(1024)S(1)}, bf16[1024,1024]{1,0:T(8,128)(2,1)S(1)}) %tuple.70), branch_computations={%region_2.3_spmd, %region_3.5_spmd} | conditional | flops 2152727552 | bytes 2138162 | solution.py:52
  77.6 2.7 %select_reduce_fusion = f32[1024]{0:T(1024)S(1)} fusion(s32[1024]{0:T(1024)S(1)} %get-tuple-element.93, s32[1024]{0:T(1024)S(1)} %get-tuple-element.90, s32[1024]{0:T(1024)S(1)} %iota_add_fusion, s32[1024]{0:T(1024)S(1)} %dynamic_slice.13, bf16[1024,1024]{1,0:T(8,128)(2,1)S(1)} %get-tuple-element.94), kind=kOutput, calls=%fused_computation.2 | convolution fusion | flops 2152725504 | bytes 2117632 | tf_op jit(solution)/shard_map/cond/branch_1_fun/dot_general | solution.py:32
  80.4 17.8 %collective-permute-done = bf16[1024,1024]{1,0:T(8,128)(2,1)} collective-permute-done((bf16[1024,1024]{1,0:T(8,128)(2,1)S(1)}, bf16[1024,1024]{1,0:T(8,128)(2,1)}, u32[]{:S(2)}, u32[]{:S(2)}) %collective-permute-start) | collective-permute-done | bytes 2097184 | tf_op jit(solution)/shard_map/ppermute | solution.py:10
  98.2 5.2 %collective-permute-done.1 = bf16[1024,1024]{1,0:T(8,128)(2,1)} collective-permute-done((bf16[1024,1024]{1,0:T(8,128)(2,1)S(1)}, bf16[1024,1024]{1,0:T(8,128)(2,1)}, u32[]{:S(2)}, u32[]{:S(2)}) %collective-permute-start.1) | collective-permute-done | bytes 2097184 | tf_op jit(solution)/shard_map/ppermute | solution.py:10
  103.4 4.2 %conditional.7 = (f32[1024]{0:T(1024)S(1)}) conditional(s32[]{:T(128)} %convert_element_type.26, f32[1024]{0:T(1024)S(1)} %get-tuple-element.145, (s32[1024]{0:T(1024)S(1)}, s32[]{:T(128)}, s32[16384]{0:T(1024)S(1)}, s32[1024]{0:T(1024)S(1)}, bf16[1024,1024]{1,0:T(8,128)(2,1)S(1)}, /*index=5*/bf16[1024,1024]{1,0:T(8,128)(2,1)}, ...), branch_computations={%region_8.9_spmd, %region_9.11_spmd} | conditional | flops 2152727552 | bytes 4239410 | solution.py:52
  103.5 4.1 %select_reduce_fusion.2 = f32[1024]{0:T(1024)S(1)} fusion(s32[1024]{0:T(1024)S(1)} %get-tuple-element.106, s32[1024]{0:T(1024)S(1)} %get-tuple-element.103, s32[1024]{0:T(1024)S(1)} %iota_add_fusion.2, s32[1024]{0:T(1024)S(1)} %dynamic_slice.23, bf16[1024,1024]{1,0:T(8,128)(2,1)S(1)} %get-tuple-element.107, bf16[1024,1024]{1,0:T(8,128)(2,1)} %get-tuple-element.108), kind=kOutput, calls=%fused_computation.7 | convolution fusion | flops 2152725504 | bytes 4214784 | tf_op jit(solution)/shard_map/cond/branch_1_fun/dot_general | solution.py:32
  107.6 35.5 %collective-permute-done.2 = bf16[1024,1024]{1,0:T(8,128)(2,1)} collective-permute-done((bf16[1024,1024]{1,0:T(8,128)(2,1)S(1)}, bf16[1024,1024]{1,0:T(8,128)(2,1)}, u32[]{:S(2)}, u32[]{:S(2)}) %collective-permute-start.2) | collective-permute-done | bytes 2097184 | tf_op jit(solution)/shard_map/ppermute | solution.py:10
  143.1 48.7 %collective-permute-done.3 = bf16[1024,1024]{1,0:T(8,128)(2,1)} collective-permute-done((bf16[1024,1024]{1,0:T(8,128)(2,1)S(1)}, bf16[1024,1024]{1,0:T(8,128)(2,1)}, u32[]{:S(2)}, u32[]{:S(2)}) %collective-permute-start.3) | collective-permute-done | bytes 2097184 | tf_op jit(solution)/shard_map/ppermute | solution.py:10
  191.8 4.2 %conditional.9 = (f32[1024]{0:T(1024)S(1)}) conditional(s32[]{:T(128)} %convert_element_type.24, f32[1024]{0:T(1024)S(1)} %get-tuple-element.147, (s32[1024]{0:T(1024)S(1)}, s32[]{:T(128)}, s32[16384]{0:T(1024)S(1)}, s32[1024]{0:T(1024)S(1)}, bf16[1024,1024]{1,0:T(8,128)(2,1)S(1)}, /*index=5*/bf16[1024,1024]{1,0:T(8,128)(2,1)}, ...), branch_computations={%region_14.15_spmd, %region_15.17_spmd} | conditional | flops 2152727552 | bytes 4239410 | solution.py:52
  191.9 4.1 %select_reduce_fusion.4 = f32[1024]{0:T(1024)S(1)} fusion(s32[1024]{0:T(1024)S(1)} %get-tuple-element.120, s32[1024]{0:T(1024)S(1)} %get-tuple-element.117, s32[1024]{0:T(1024)S(1)} %iota_add_fusion.4, s32[1024]{0:T(1024)S(1)} %dynamic_slice.25, bf16[1024,1024]{1,0:T(8,128)(2,1)S(1)} %get-tuple-element.121, bf16[1024,1024]{1,0:T(8,128)(2,1)} %get-tuple-element.122), kind=kOutput, calls=%fused_computation.11 | convolution fusion | flops 2152725504 | bytes 4214784 | tf_op jit(solution)/shard_map/cond/branch_1_fun/dot_general | solution.py:32
  196.1 25.3 %all_to_all.25 = f32[128,8,1]{1,2,0:T(1,128)S(1)} all-to-all(f32[128,8,1]{1,2,0:T(1,128)S(1)} %bitcast.29), channel_id=1, replica_groups=mesh['group'=8,'block'=16] {'group','block'}, dimensions={0} | all-to-all | bytes 8192 | tf_op jit(solution)/shard_map/all_to_all | solution.py:62
  221.8 0.8 reduce.3
  222.8 8.8 %gather_fusion = f32[1024]{0:T(1024)} fusion(f32[1024]{0:T(1024)S(1)} %all_to_all.21, s32[1024]{0:T(1024)S(1)} %get-tuple-element.123), kind=kCustom, calls=%fused_computation | custom fusion | bytes 12288 | tf_op jit(solution)/shard_map/gather | solution.py:63
  (21 shorter events, 1.0 us)
Async XLA Ops:
  0.0 2.9 %copy-start = (bf16[1024,1024]{1,0:T(8,128)(2,1)S(1)}, bf16[1024,1024]{1,0:T(8,128)(2,1)}, u32[]{:S(2)}) copy-start(bf16[1024,1024]{1,0:T(8,128)(2,1)} %param.13) | copy-start | bytes 6291460
  10.2 52.7 %copy-start.1 = (s32[16384]{0:T(1024)S(1)}, s32[16384]{0:T(1024)}, u32[]{:S(2)}) copy-start(s32[16384]{0:T(1024)} %param.15) | copy-start | bytes 196612
  51.0 47.2 %collective-permute-start = (bf16[1024,1024]{1,0:T(8,128)(2,1)S(1)}, bf16[1024,1024]{1,0:T(8,128)(2,1)}, u32[]{:S(2)}, u32[]{:S(2)}) collective-permute-start(bf16[1024,1024]{1,0:T(8,128)(2,1)S(1)} %bitcast.20), channel_id=1, source_target_pairs={{0,1},{1,2},{2,3},{3,4},{4,5},{5,6},{6,7},{7,8},{8,9},{9,10},{10,1... | collective-permute-start | bytes 6291464 | tf_op jit(solution)/shard_map/ppermute | solution.py:10
  55.3 48.1 %collective-permute-start.1 = (bf16[1024,1024]{1,0:T(8,128)(2,1)S(1)}, bf16[1024,1024]{1,0:T(8,128)(2,1)}, u32[]{:S(2)}, u32[]{:S(2)}) collective-permute-start(bf16[1024,1024]{1,0:T(8,128)(2,1)S(1)} %bitcast.21), channel_id=1, source_target_pairs={{1,0},{2,1},{3,2},{4,3},{5,4},{6,5},{7,6},{8,7},{9,8},{10,9},{11,1... | collective-permute-start | bytes 6291464 | tf_op jit(solution)/shard_map/ppermute | solution.py:10
  56.6 86.5 %collective-permute-start.2 = (bf16[1024,1024]{1,0:T(8,128)(2,1)S(1)}, bf16[1024,1024]{1,0:T(8,128)(2,1)}, u32[]{:S(2)}, u32[]{:S(2)}) collective-permute-start(bf16[1024,1024]{1,0:T(8,128)(2,1)S(1)} %bitcast.22), channel_id=1, source_target_pairs={{0,2},{1,3},{2,4},{3,5},{4,6},{5,7},{6,8},{7,9},{8,10},{9,11},{10,... | collective-permute-start | bytes 6291464 | tf_op jit(solution)/shard_map/ppermute | solution.py:10
  61.6 130.2 %collective-permute-start.3 = (bf16[1024,1024]{1,0:T(8,128)(2,1)S(1)}, bf16[1024,1024]{1,0:T(8,128)(2,1)}, u32[]{:S(2)}, u32[]{:S(2)}) collective-permute-start(bf16[1024,1024]{1,0:T(8,128)(2,1)S(1)} %bitcast.23), channel_id=1, source_target_pairs={{2,0},{3,1},{4,2},{5,3},{6,4},{7,5},{8,6},{9,7},{10,8},{11,9},{12,... | collective-permute-start | bytes 6291464 | tf_op jit(solution)/shard_map/ppermute | solution.py:10
where the time goes:
time: 232 us
  waiting for transfers between devices  107 us (46%)
  blocking collectives  66 us (28%)
  between operations  12.8 us (6%)
  starting transfers between devices  11.9 us (5%)
  local copies, waits for them, and re-layouts  11.6 us (5%)
  other arithmetic  11 us (5%)
  matrix products  10.9 us (5%)
    ppermute x4, waiting for transfers between devices, passed_along(): return lax.ppermute(x, axis, pairs)  107 us
    all_to_all x1, blocking collectives, body(): lax.all_to_all(outgoing, ('group', 'block'), split_axis=0, concat_axis=0,...  40.8 us
    all_to_all x1, blocking collectives, body(): lax.all_to_all(row_best, ('group', 'block'), split_axis=0, concat_axis=0,...  25.3 us
    ppermute x4, starting transfers between devices, passed_along(): return lax.ppermute(x, axis, pairs)  11.9 us
    dot_general x3, matrix products, masked_gram(): lax.dot_general(received, piece, (((1,), (1,)), ((), ())), preferred_elem...  10.9 us
    gather x1, local copies, waits for them, and re-layouts, body(): return returned[position]  8.84 us
    scatter x1, other arithmetic, body(): outgoing = jnp.zeros_like(unit).at[position].set(unit)  7.24 us
  transfers between devices with their start and end apart: 4, of which 4 were waited for; matrix products, arithmetic and copies ran while one was open for 4% of the time, Pallas kernels for 0%

commit v1 on v0

--- a/solution.py
+++ b/solution.py
@@ -1,7 +1,61 @@
 import jax
 import jax.numpy as jnp
 from jax import lax
+from jax.experimental import pallas as pl
+from jax.experimental.pallas import tpu as pltpu
 from jax.sharding import PartitionSpec as P
+
+MESH = pl.DeviceIdType.MESH
+
+
+def exchange_kernel(src, dst, send_sem, recv_sem, own_sem):
+    blocks = lax.axis_size("block")
+    devices = lax.axis_size("group") * blocks
+    me = lax.axis_index("group") * blocks + lax.axis_index("block")
+    barrier = pltpu.get_barrier_semaphore()
+
+    def greet(j, _):
+        peer = lax.rem(me + j, devices)
+        pl.semaphore_signal(
+            barrier, inc=1, device_id=(peer // blocks, lax.rem(peer, blocks)), device_id_type=MESH
+        )
+        return 0
+
+    lax.fori_loop(1, devices, greet, 0)
+    pl.semaphore_wait(barrier, devices - 1)
+    own = pltpu.make_async_copy(src.at[me], dst.at[me], own_sem)
+    own.start()
+
+    def send(j, _):
+        peer = lax.rem(me + j, devices)
+        pltpu.make_async_remote_copy(
+            src.at[peer],
+            dst.at[me],
+            send_sem,
+            recv_sem,
+            device_id=(peer // blocks, lax.rem(peer, blocks)),
+            device_id_type=MESH,
+        ).start()
+        return 0
+
+    lax.fori_loop(1, devices, send, 0)
+    own.wait()
+    part = src.at[pl.ds(0, devices - 1)]
+    pltpu.make_async_copy(part, part, send_sem).wait()
+    pltpu.make_async_copy(part, part, recv_sem).wait()
+
+
+def exchange(x, collective_id):
+    return pl.pallas_call(
+        exchange_kernel,
+        out_shape=jax.ShapeDtypeStruct(x.shape, x.dtype),
+        in_specs=[pl.BlockSpec(memory_space=pltpu.VMEM)],
+        out_specs=pl.BlockSpec(memory_space=pltpu.VMEM),
+        scratch_shapes=[pltpu.SemaphoreType.DMA] * 3,
+        compiler_params=pltpu.CompilerParams(
+            collective_id=collective_id, has_side_effects=True, vmem_limit_bytes=32 * 2**20
+        ),
+    )(x)
 
 
 def passed_along(x, axis, by):
@@ -14,14 +68,15 @@
     rows = embeddings.shape[0]
     groups = lax.axis_size("group")
     blocks = lax.axis_size("block")
-    slot = rows // (groups * blocks)
+    devices = groups * blocks
+    slot = rows // devices
     block_id = lax.axis_index("block")
     values = embeddings.astype(jnp.float32)
     squares = jnp.sum(values * values, axis=1, keepdims=True)
     unit = (values * lax.rsqrt(squares + 1e-06)).astype(jnp.bfloat16)
     position = target // rows * slot + target % slot
     outgoing = jnp.zeros_like(unit).at[position].set(unit)
-    received = lax.all_to_all(outgoing, ("group", "block"), split_axis=0, concat_axis=0, tiled=True)
+    received = exchange(outgoing.reshape(devices, slot, -1), 0).reshape(rows, -1)
     own_start = block_id * rows
     own_labels = lax.dynamic_slice_in_dim(cluster_labels, own_start, rows, 0)
     own_rows = own_start + jnp.arange(rows, dtype=jnp.int32)
@@ -59,8 +114,10 @@
         valid = (source >= 0) & (source < blocks)
         start = jnp.clip(source, 0, blocks - 1) * rows
         row_best = add_tile(row_best, other, start, valid)
-    returned = lax.all_to_all(row_best, ("group", "block"), split_axis=0, concat_axis=0, tiled=True)
-    return returned[position]
+    chunks = jnp.broadcast_to(row_best.reshape(groups, 1, 1, -1), (groups, blocks, 1, rows // groups))
+    returned = exchange(chunks.reshape(devices, 1, rows // groups), 1)
+    mine = lax.dynamic_slice_in_dim(returned[:, 0], block_id * slot, slot, 1)
+    return mine.reshape(rows)[position]
 
 
 def solution(mesh):

time: 232 us -> 231 us (level)
  Pallas kernels: 0 us -> 70 us
  blocking collectives: 66 us -> 0 us
  matrix products: 10.9 us -> 14.2 us
  starting transfers between devices: 11.9 us -> 8.7 us
    pallas_call x0 -> x2, Pallas kernels: none -> 70 us  [exchange(): pl.pallas_call(exchange_kernel, out_shape=jax.ShapeDtypeStruct(x.shape, x...]
    all_to_all x2 -> x0, blocking collectives: 66 us -> none  [the longest x1 40.8 us: body(): lax.all_to_all(outgoing, ('group', 'block'), split_axis=0, concat_axis=0,...]
    dot_general x3, matrix products: 10.9 us -> 14.2 us  [masked_gram(): lax.dot_general(received, piece, (((1,), (1,)), ((), ())), preferred_elem...]
    ppermute x4, starting transfers between devices: 11.9 us -> 8.7 us  [passed_along(): return lax.ppermute(x, axis, pairs)]
    ppermute x4, waiting for transfers between devices: 107 us -> 105 us  [passed_along(): return lax.ppermute(x, axis, pairs)]
  transfers between devices with their start and end apart: 4 -> 4, of which waited for: 4 -> 4; matrix products, arithmetic and copies ran while one was open for 4% -> 5% of each run, Pallas kernels for 0% -> 0%
where the time goes in v1:
time: 231 us
  waiting for transfers between devices  105 us (45%)
  Pallas kernels  70 us (30%)
  matrix products  14.2 us (6%)
  between operations  12.2 us (5%)
  local copies, waits for them, and re-layouts  11.3 us (5%)
  other arithmetic  9.66 us (4%)
  starting transfers between devices  8.7 us (4%)
    ppermute x4, waiting for transfers between devices, passed_along(): return lax.ppermute(x, axis, pairs)  105 us
    pallas_call x2, Pallas kernels, exchange(): pl.pallas_call(exchange_kernel, out_shape=jax.ShapeDtypeStruct(x.shape, x...  70 us
    dot_general x3, matrix products, masked_gram(): lax.dot_general(received, piece, (((1,), (1,)), ((), ())), preferred_elem...  14.2 us
    gather x1, local copies, waits for them, and re-layouts, body(): return mine.reshape(rows)[position]  8.84 us
    ppermute x4, starting transfers between devices, passed_along(): return lax.ppermute(x, axis, pairs)  8.7 us
    scatter x1, other arithmetic, body(): outgoing = jnp.zeros_like(unit).at[position].set(unit)  6.85 us
  transfers between devices with their start and end apart: 4, of which 4 were waited for; matrix products, arithmetic and copies ran while one was open for 5% of the time, Pallas kernels for 0%

profile of v1, /device:TPU:1, one launch (start us, length us, event | category | flops | bytes accessed | tf_op | source)
XLA Modules:
  0.0 230.6 jit_solution(9693412037923621194)
XLA Ops:
  0.0 0.7 broadcast_clamp_fusion
  0.7 2.1 fusion
  2.8 6.9 %scatter_custom_fusion = bf16[1024,1024]{1,0:T(8,128)(2,1)S(1)} fusion(s32[1024]{0:T(1024)S(1)} %get-tuple-element.124, bf16[1024,1024]{1,0:T(8,128)(2,1)} %param.13, f32[1024]{0:T(1024)S(1)} %add_rsqrt_fusion, bf16[]{:T(256)} %constant.99.clone.1), kind=kCustom, calls=%fused_computation.17 | custom fusion | flops 3145728 | bytes 4198402 | tf_op jit(solution)/shard_map/scatter | solution.py:78
  9.7 40.9 %shard_map.37 = bf16[128,8,1024]{2,1,0:T(8,128)(2,1)} custom-call(bf16[128,8,1024]{2,1,0:T(8,128)(2,1)S(1)} %bitcast.19), custom_call_target="tpu_custom_call" | custom-call | tf_op jit(solution)/shard_map/pallas_call | solution.py:49
  50.6 2.7 %collective-permute-start = (bf16[1024,1024]{1,0:T(8,128)(2,1)}, bf16[1024,1024]{1,0:T(8,128)(2,1)}, u32[]{:S(2)}, u32[]{:S(2)}) collective-permute-start(bf16[1024,1024]{1,0:T(8,128)(2,1)} %bitcast.6), channel_id=1, source_target_pairs={{0,1},{1,2},{2,3},{3,4},{4,5},{5,6},{6,7},{7,8},{8,9},{9,10},{10,1... | collective-permute-start | bytes 6291464 | tf_op jit(solution)/shard_map/ppermute | solution.py:64
  53.3 1.3 collective-permute-start.1
  54.6 3.4 %collective-permute-start.2 = (bf16[1024,1024]{1,0:T(8,128)(2,1)}, bf16[1024,1024]{1,0:T(8,128)(2,1)}, u32[]{:S(2)}, u32[]{:S(2)}) collective-permute-start(bf16[1024,1024]{1,0:T(8,128)(2,1)} %bitcast.6), channel_id=1, source_target_pairs={{0,2},{1,3},{2,4},{3,5},{4,6},{5,7},{6,8},{7,9},{8,10},{9,11},{10,... | collective-permute-start | bytes 6291464 | tf_op jit(solution)/shard_map/ppermute | solution.py:64
  58.0 1.3 collective-permute-start.3
  59.4 0.6 fusion.14
  62.3 0.6 fusion.16
  67.8 0.6 fusion.12
  73.3 4.9 %conditional.5 = (f32[1024]{0:T(1024)S(1)}) conditional(s32[]{:T(128)} %bitcast.4, () %tuple.35, (s32[1024]{0:T(1024)S(1)}, s32[]{:T(128)}, s32[16384]{0:T(1024)S(1)}, s32[1024]{0:T(1024)S(1)}, bf16[1024,1024]{1,0:T(8,128)(2,1)}) %tuple.65), branch_computations={%region_2.3_spmd, %region_3.5_spmd} | conditional | flops 2152727552 | bytes 2138162 | solution.py:107
  73.4 4.7 %select_reduce_fusion = f32[1024]{0:T(1024)S(1)} fusion(s32[1024]{0:T(1024)S(1)} %get-tuple-element.93, s32[1024]{0:T(1024)S(1)} %get-tuple-element.90, s32[1024]{0:T(1024)S(1)} %iota_add_fusion, s32[1024]{0:T(1024)S(1)} %dynamic_slice.13, bf16[1024,1024]{1,0:T(8,128)(2,1)} %get-tuple-element.94), kind=kOutput, calls=%fused_computation.2 | convolution fusion | flops 2152725504 | bytes 2117632 | tf_op jit(solution)/shard_map/cond/branch_1_fun/dot_general | solution.py:87
  78.1 19.0 %collective-permute-done = bf16[1024,1024]{1,0:T(8,128)(2,1)} collective-permute-done((bf16[1024,1024]{1,0:T(8,128)(2,1)}, bf16[1024,1024]{1,0:T(8,128)(2,1)}, u32[]{:S(2)}, u32[]{:S(2)}) %collective-permute-start) | collective-permute-done | bytes 2097184 | tf_op jit(solution)/shard_map/ppermute | solution.py:64
  97.1 5.2 %collective-permute-done.1 = bf16[1024,1024]{1,0:T(8,128)(2,1)} collective-permute-done((bf16[1024,1024]{1,0:T(8,128)(2,1)}, bf16[1024,1024]{1,0:T(8,128)(2,1)}, u32[]{:S(2)}, u32[]{:S(2)}) %collective-permute-start.1) | collective-permute-done | bytes 2097184 | tf_op jit(solution)/shard_map/ppermute | solution.py:64
  102.3 4.8 %conditional.7 = (f32[1024]{0:T(1024)S(1)}) conditional(s32[]{:T(128)} %convert_element_type.26, f32[1024]{0:T(1024)S(1)} %get-tuple-element.145, (s32[1024]{0:T(1024)S(1)}, s32[]{:T(128)}, s32[16384]{0:T(1024)S(1)}, s32[1024]{0:T(1024)S(1)}, bf16[1024,1024]{1,0:T(8,128)(2,1)}, /*index=5*/bf16[1024,1024]{1,0:T(8,128)(2,1)}, f32[1024]{0:T(1024)S(1)}) %tuple.67), branch_computations={%region_8.9_spmd, %region_9.11_spmd} | conditional | flops 2152727552 | bytes 4239410 | solution.py:107
  102.4 4.7 %select_reduce_fusion.2 = f32[1024]{0:T(1024)S(1)} fusion(s32[1024]{0:T(1024)S(1)} %get-tuple-element.106, s32[1024]{0:T(1024)S(1)} %get-tuple-element.103, s32[1024]{0:T(1024)S(1)} %iota_add_fusion.2, s32[1024]{0:T(1024)S(1)} %dynamic_slice.25, bf16[1024,1024]{1,0:T(8,128)(2,1)} %get-tuple-element.107, bf16[1024,1024]{1,0:T(8,128)(2,1)} %get-tuple-element.108), kind=kOutput, calls=%fused_computation.7 | convolution fusion | flops 2152725504 | bytes 4214784 | tf_op jit(solution)/shard_map/cond/branch_1_fun/dot_general | solution.py:87
  107.1 34.9 %collective-permute-done.2 = bf16[1024,1024]{1,0:T(8,128)(2,1)} collective-permute-done((bf16[1024,1024]{1,0:T(8,128)(2,1)}, bf16[1024,1024]{1,0:T(8,128)(2,1)}, u32[]{:S(2)}, u32[]{:S(2)}) %collective-permute-start.2) | collective-permute-done | bytes 2097184 | tf_op jit(solution)/shard_map/ppermute | solution.py:64
  142.1 45.5 %collective-permute-done.3 = bf16[1024,1024]{1,0:T(8,128)(2,1)} collective-permute-done((bf16[1024,1024]{1,0:T(8,128)(2,1)}, bf16[1024,1024]{1,0:T(8,128)(2,1)}, u32[]{:S(2)}, u32[]{:S(2)}) %collective-permute-start.3) | collective-permute-done | bytes 2097184 | tf_op jit(solution)/shard_map/ppermute | solution.py:64
  187.5 4.8 %conditional.9 = (f32[1024]{0:T(1024)S(1)}) conditional(s32[]{:T(128)} %convert_element_type.24, f32[1024]{0:T(1024)S(1)} %get-tuple-element.147, (s32[1024]{0:T(1024)S(1)}, s32[]{:T(128)}, s32[16384]{0:T(1024)S(1)}, s32[1024]{0:T(1024)S(1)}, bf16[1024,1024]{1,0:T(8,128)(2,1)}, /*index=5*/bf16[1024,1024]{1,0:T(8,128)(2,1)}, ...), branch_computations={%region_14.15_spmd, %region_15.17_spmd} | conditional | flops 2152727552 | bytes 4239410 | solution.py:107
  187.6 4.7 %select_reduce_fusion.4 = f32[1024]{0:T(1024)S(1)} fusion(s32[1024]{0:T(1024)S(1)} %get-tuple-element.120, s32[1024]{0:T(1024)S(1)} %get-tuple-element.117, s32[1024]{0:T(1024)S(1)} %iota_add_fusion.4, s32[1024]{0:T(1024)S(1)} %dynamic_slice.27, bf16[1024,1024]{1,0:T(8,128)(2,1)} %get-tuple-element.121, bf16[1024,1024]{1,0:T(8,128)(2,1)} %get-tuple-element.122), kind=kOutput, calls=%fused_computation.11 | convolution fusion | flops 2152725504 | bytes 4214784 | tf_op jit(solution)/shard_map/cond/branch_1_fun/dot_general | solution.py:87
  192.4 29.1 %shard_map.38 = f32[128,1,128]{2,1,0:T(1,128)S(1)} custom-call(f32[128,1,128]{2,1,0:T(1,128)S(1)} %bitcast.20), custom_call_target="tpu_custom_call" | custom-call | tf_op jit(solution)/shard_map/pallas_call | solution.py:49
  221.5 0.2 dynamic-slice_reduce_fusion
  221.8 8.8 %gather_fusion = f32[1024]{0:T(1024)} fusion(f32[1024]{0:T(1024)S(1)} %reshape.79, s32[1024]{0:T(1024)S(1)} %get-tuple-element.123), kind=kCustom, calls=%fused_computation | custom fusion | bytes 12288 | tf_op jit(solution)/shard_map/gather | solution.py:120
  (18 shorter events, 0.4 us)
Async XLA Ops:
  9.6 49.7 %copy-start = (s32[16384]{0:T(1024)S(1)}, s32[16384]{0:T(1024)}, u32[]{:S(2)}) copy-start(s32[16384]{0:T(1024)} %param.15) | copy-start | bytes 196612
  50.6 46.5 %collective-permute-start = (bf16[1024,1024]{1,0:T(8,128)(2,1)}, bf16[1024,1024]{1,0:T(8,128)(2,1)}, u32[]{:S(2)}, u32[]{:S(2)}) collective-permute-start(bf16[1024,1024]{1,0:T(8,128)(2,1)} %bitcast.6), channel_id=1, source_target_pairs={{0,1},{1,2},{2,3},{3,4},{4,5},{5,6},{6,7},{7,8},{8,9},{9,10},{10,1... | collective-permute-start | bytes 6291464 | tf_op jit(solution)/shard_map/ppermute | solution.py:64
  53.3 49.0 %collective-permute-start.1 = (bf16[1024,1024]{1,0:T(8,128)(2,1)}, bf16[1024,1024]{1,0:T(8,128)(2,1)}, u32[]{:S(2)}, u32[]{:S(2)}) collective-permute-start(bf16[1024,1024]{1,0:T(8,128)(2,1)} %bitcast.6), channel_id=1, source_target_pairs={{1,0},{2,1},{3,2},{4,3},{5,4},{6,5},{7,6},{8,7},{9,8},{10,9},{11,1... | collective-permute-start | bytes 6291464 | tf_op jit(solution)/shard_map/ppermute | solution.py:64
  54.6 87.5 %collective-permute-start.2 = (bf16[1024,1024]{1,0:T(8,128)(2,1)}, bf16[1024,1024]{1,0:T(8,128)(2,1)}, u32[]{:S(2)}, u32[]{:S(2)}) collective-permute-start(bf16[1024,1024]{1,0:T(8,128)(2,1)} %bitcast.6), channel_id=1, source_target_pairs={{0,2},{1,3},{2,4},{3,5},{4,6},{5,7},{6,8},{7,9},{8,10},{9,11},{10,... | collective-permute-start | bytes 6291464 | tf_op jit(solution)/shard_map/ppermute | solution.py:64
  58.0 129.5 %collective-permute-start.3 = (bf16[1024,1024]{1,0:T(8,128)(2,1)}, bf16[1024,1024]{1,0:T(8,128)(2,1)}, u32[]{:S(2)}, u32[]{:S(2)}) collective-permute-start(bf16[1024,1024]{1,0:T(8,128)(2,1)} %bitcast.6), channel_id=1, source_target_pairs={{2,0},{3,1},{4,2},{5,3},{6,4},{7,5},{8,6},{9,7},{10,8},{11,9},{12,... | collective-permute-start | bytes 6291464 | tf_op jit(solution)/shard_map/ppermute | solution.py:64

commit v2 on v0

v2 whole, which is shorter than its diff:
```python
import jax
import jax.numpy as jnp
from jax import lax
from jax.experimental import pallas as pl
from jax.experimental.pallas import tpu as pltpu
from jax.sharding import PartitionSpec as P

MESH = pl.DeviceIdType.MESH
E = 1024
ROWS = 1024
GROUPS = 8
BLOCKS = 16
DEVICES = GROUPS * BLOCKS
SLOT = ROWS // DEVICES
PIECE = ROWS // GROUPS
LOW = -2.0


def home_device(target):
    block = target // ROWS
    group, place = block // BLOCKS, block % BLOCKS
    x, half = group // 2, group % 2
    p, core = place // 2, place % 2
    turn, y = p // 4, p % 4
    y = jnp.where(turn == 1, 3 - y, y)
    return (2 * x + core) * BLOCKS + (2 * half + turn) * 4 + y


def kernel(
    emb, tgt, lab, out,
    raw, unit, outgoing, recv, own, sib, nb, lab_loc, lab_in, part_out, part_in, score, back, lanes,
    raw_sem, lab_sem, self_sem, lab_ss, lab_rs, a2a_ss, a2a_rs, sib_ss, sib_rs, nb_ss, nb_rs,
    part_ss, part_rs, back_ss, back_rs,
):
    gme = lax.axis_index("group")
    bme = lax.axis_index("block")
    me = gme * BLOCKS + bme
    core = lax.rem(gme, 2)
    sibling = gme + 1 - 2 * core
    z, y = bme // 4, lax.rem(bme, 4)
    half, turn = z // 2, lax.rem(z, 2)
    p = turn * 4 + y + turn * (3 - 2 * y)

    def at_place(q):
        q = jnp.clip(q, 0, 7)
        t, r = q // 4, lax.rem(q, 4)
        return (2 * half + t) * 4 + r + t * (3 - 2 * r)

    p_to = p - 1 + 2 * core
    p_from = p + 1 - 2 * core
    has_to = (p_to >= 0) & (p_to < 8)
    has_from = (p_from >= 0) & (p_from < 8)
    dev_to = (gme, at_place(p_to))
    dev_from = (gme, at_place(p_from))
    dev_sib = (sibling, bme)

    for t in range(GROUPS):
        part_in[0, t] = jnp.full((1, PIECE), LOW, jnp.float32)
        part_in[2, t] = jnp.full((1, PIECE), LOW, jnp.float32)
    raw_copies = []
    for i in range(4):
        rows = pl.ds(i * 256, 256)
        copy = pltpu.make_async_copy(emb.at[rows], raw.at[rows], raw_sem.at[i])
        copy.start()
        raw_copies.append(copy)
    lab_copies = []
    for i in range(4):
        place = jnp.clip(2 * p - 1 + i, 0, BLOCKS - 1)
        copy = pltpu.make_async_copy(lab.at[place], lab_loc.at[i], lab_sem.at[i])
        copy.start()
        lab_copies.append(copy)

    barrier = pltpu.get_barrier_semaphore()

    def greet(j, _):
        peer = lax.rem(me + j, DEVICES)
        pl.semaphore_signal(
            barrier, inc=1, device_id=(peer // BLOCKS, lax.rem(peer, BLOCKS)), device_id_type=MESH
        )
        return 0

    lax.fori_loop(1, DEVICES, greet, 0, unroll=False)

    for i in range(4):
        raw_copies[i].wait()
        for j in range(2):
            rows = pl.ds(i * 256 + j * 128, 128)
            values = raw[rows, :].astype(jnp.float32)
            squares = jnp.sum(values * values, axis=1, keepdims=True)
            unit[rows, :] = (values * lax.rsqrt(squares + 1e-06)).astype(jnp.bfloat16)

    target = tgt[...]
    home = home_device(target)
    position = home * SLOT + target % SLOT
    row_iota = lax.broadcasted_iota(jnp.int32, (PIECE, ROWS), 0)

    def permute(q, _):
        piece = lax.rem(gme + q, GROUPS)
        onehot = jnp.where(row_iota == position - piece * PIECE, 1.0, 0.0).astype(jnp.bfloat16)
        picked = jnp.dot(onehot, unit[...], preferred_element_type=jnp.float32)
        outgoing[pl.ds(piece * BLOCKS, BLOCKS)] = picked.reshape(BLOCKS, SLOT, E).astype(jnp.bfloat16)
        return 0

    lax.fori_loop(0, GROUPS, permute, 0, unroll=False)
    for copy in lab_copies:
        copy.wait()

    pl.semaphore_wait(barrier, DEVICES - 1)

    lab_copy = pltpu.make_async_remote_copy(
        lab_loc, lab_in, lab_ss, lab_rs, device_id=dev_sib, device_id_type=MESH
    )
    lab_copy.start()
    self_copy = pltpu.make_async_copy(outgoing.at[me], recv.at[me], self_sem)
    self_copy.start()

    def send_stage(q, _):
        to_group = lax.rem(gme + q, GROUPS)

        def send(i, _):
            to_block = lax.rem(bme + i, BLOCKS)
            pltpu.make_async_remote_copy(
                outgoing.at[to_group * BLOCKS + to_block],
                recv.at[me],
                a2a_ss,
                a2a_rs.at[q],
                device_id=(to_group, to_block),
                device_id_type=MESH,
            ).start()
            return 0

        lax.fori_loop(jnp.where(q == 0, 1, 0), BLOCKS, send, 0, unroll=False)
        return 0

    lax.fori_loop(0, GROUPS, send_stage, 0, unroll=False)

    lab_copy.wait()
    local_labels = half == core
    labels = [
        jnp.where(local_labels, lab_loc[i], lab_in[i]).astype(jnp.float32) for i in range(4)
    ]
    is0 = core == 0
    own_lab = jnp.where(is0, labels[1], labels[2])
    sib_lab = jnp.where(is0, labels[2], labels[1])
    nb_lab = jnp.where(is0, labels[3], labels[0])
    for t in range(GROUPS):
        cut = slice(t * PIECE, (t + 1) * PIECE)
        lanes[0, t] = own_lab[:, cut]
        lanes[1, t] = nb_lab[:, cut]

    def forward(piece, peer, dst, ss, rs):
        rows = pl.ds(piece * PIECE, PIECE)
        return pltpu.make_async_remote_copy(
            own.at[rows], dst.at[rows], ss, rs, device_id=peer, device_id_type=MESH
        )

    def arrive(q, _):
        piece = lax.rem(gme - q + GROUPS, GROUPS)

        @pl.when(q == 0)
        def _():
            self_copy.wait()
            part = recv.at[pl.ds(0, BLOCKS - 1)]
            pltpu.make_async_copy(part, part, a2a_rs.at[0]).wait()

        @pl.when(q > 0)
        def _():
            part = recv.at[pl.ds(0, BLOCKS)]
            pltpu.make_async_copy(part, part, a2a_rs.at[q]).wait()

        got = recv[pl.ds(piece * BLOCKS, BLOCKS)].astype(jnp.float32)
        own[pl.ds(piece * PIECE, PIECE), :] = got.reshape(PIECE, E).astype(jnp.bfloat16)

        @pl.when(has_to)
        def _():
            forward(piece, dev_to, nb, nb_ss, nb_rs.at[q]).start()

        forward(piece, dev_sib, sib, sib_ss, sib_rs).start()
        return 0

    lax.fori_loop(0, GROUPS, arrive, 0, unroll=False)

    def row_labels(which, piece):
        wide = jnp.broadcast_to(lanes[which, piece], (PIECE, PIECE))
        return wide.T

    def tile(a_rows, a_lab, b_ref, b_lab, col_best, diagonal):
        gram = lax.dot_general(
            a_rows, b_ref[...], (((1,), (1,)), ((), ())), preferred_element_type=jnp.float32
        )
        rows_best = jnp.full((PIECE, PIECE), LOW, jnp.float32)
        new = []
        for t in range(GROUPS):
            cut = slice(t * PIECE, (t + 1) * PIECE)
            same = a_lab == b_lab[:, cut]
            if diagonal is not None:
                r = lax.broadcasted_iota(jnp.int32, (PIECE, PIECE), 0) + diagonal * PIECE
                c = lax.broadcasted_iota(jnp.int32, (PIECE, PIECE), 1) + t * PIECE
                same = same & (r != c)
            masked = jnp.where(same, gram[:, cut], LOW)
            rows_best = jnp.maximum(rows_best, masked)
            new.append(jnp.max(masked.reshape(PIECE // 8, 8, PIECE), axis=0))
        return jnp.maximum(col_best, jnp.concatenate(new, axis=1)), rows_best

    def to_lanes(rows_best):
        return jnp.max(rows_best.T, axis=0, keepdims=True)

    start_best = jnp.full((8, ROWS), LOW, jnp.float32)

    def own_tile(q, best):
        rows = own[pl.ds(q * PIECE, PIECE), :]
        best, _ = tile(rows, row_labels(0, q), own, own_lab, best, q)
        return best

    own_best = lax.fori_loop(0, GROUPS, own_tile, start_best, unroll=False)

    pltpu.make_async_copy(sib, sib, sib_rs).wait()


    def near(q, bests):
        own_best, sib_best = bests
        piece = lax.rem(gme - q + GROUPS, GROUPS)
        rows = pl.ds(piece * PIECE, PIECE)

        def with_nb(own_best, sib_best):
            part = nb.at[rows]
            pltpu.make_async_copy(part, part, nb_rs.at[q]).wait()
            nb_rows, nb_labels = nb[rows, :], row_labels(1, piece)
            own_best, r2 = tile(nb_rows, nb_labels, own, own_lab, own_best, None)
            part_out[1, piece] = to_lanes(r2)

            return own_best, sib_best

        own_best, sib_best = lax.cond(has_from, with_nb, lambda a, b: (a, b), own_best, sib_best)

        def third0(sib_best):
            sib_best, r3 = tile(nb[rows, :], row_labels(1, piece), sib, sib_lab, sib_best, None)
            part_out[1, piece] = jnp.maximum(part_out[1, piece], to_lanes(r3))
            return sib_best

        def third1(sib_best):
            sib_best, r3 = tile(own[rows, :], row_labels(0, piece), sib, sib_lab, sib_best, None)
            part_in[2, piece] = to_lanes(r3)
            return sib_best

        sib_best = lax.cond(has_from & is0, third0, lambda a: a, sib_best)
        sib_best = lax.cond(core == 1, third1, lambda a: a, sib_best)
        return own_best, sib_best

    own_best, sib_best = lax.fori_loop(0, GROUPS, near, (own_best, start_best), unroll=False)

    own_line = jnp.max(own_best, axis=0, keepdims=True)
    sib_line = jnp.max(sib_best, axis=0, keepdims=True)
    for t in range(GROUPS):
        part_out[0, t] = sib_line[:, t * PIECE : (t + 1) * PIECE]

    to_sib = pltpu.make_async_remote_copy(
        part_out.at[0], part_in.at[1], part_ss.at[0], part_rs.at[0], device_id=dev_sib, device_id_type=MESH
    )
    to_nb = pltpu.make_async_remote_copy(
        part_out.at[1], part_in.at[0], part_ss.at[1], part_rs.at[1], device_id=dev_from, device_id_type=MESH
    )
    to_sib.start()

    @pl.when(has_from)
    def _():
        to_nb.start()

    to_sib.wait_recv()

    @pl.when(has_to)
    def _():
        to_nb.wait_recv()

    for t in range(GROUPS):
        best = jnp.maximum(own_line[:, t * PIECE : (t + 1) * PIECE], part_in[0, t])
        best = jnp.maximum(best, jnp.maximum(part_in[1, t], part_in[2, t]))
        score[t] = best

    own_back = pltpu.make_async_copy(score.at[gme], back.at[me], self_sem)
    own_back.start()

    def give(j, _):
        peer = lax.rem(me + j, DEVICES)
        pltpu.make_async_remote_copy(
            score.at[peer // BLOCKS],
            back.at[me],
            back_ss,
            back_rs,
            device_id=(peer // BLOCKS, lax.rem(peer, BLOCKS)),
            device_id_type=MESH,
        ).start()
        return 0

    lax.fori_loop(1, DEVICES, give, 0, unroll=False)

    part = outgoing.at[pl.ds(0, DEVICES - 1)]
    pltpu.make_async_copy(part, part, a2a_ss).wait()
    pltpu.make_async_copy(own, own, sib_ss).wait()

    @pl.when(has_to)
    def _():
        pltpu.make_async_copy(own, own, nb_ss).wait()

    to_sib.wait_send()

    @pl.when(has_from)
    def _():
        to_nb.wait_send()

    own_back.wait()
    part = back.at[pl.ds(0, DEVICES - 1)]
    pltpu.make_async_copy(part, part, back_ss).wait()
    pltpu.make_async_copy(part, part, back_rs).wait()

    by_lane = back[:, 0, :].T
    mine = jnp.zeros((SLOT, DEVICES), jnp.float32)
    for b in range(BLOCKS):
        mine = jnp.where(bme == b, by_lane[b * SLOT : (b + 1) * SLOT, :], mine)
    dev_iota = lax.broadcasted_iota(jnp.int32, (DEVICES, ROWS), 0)
    pick = jnp.where(dev_iota == home, 1.0, 0.0)
    slots = lax.dot_general(
        mine,
        pick,
        (((1,), (0,)), ((), ())),
        precision=lax.Precision.HIGHEST,
        preferred_element_type=jnp.float32,
    )
    slot_iota = lax.broadcasted_iota(jnp.int32, (SLOT, ROWS), 0)
    out[...] = jnp.sum(jnp.where(slot_iota == target % SLOT, slots, 0.0), axis=0, keepdims=True)


def body(embeddings, target, cluster_labels):
    bf, f32, i32 = jnp.bfloat16, jnp.float32, jnp.int32
    dma = pltpu.SemaphoreType.DMA
    result = pl.pallas_call(
        kernel,
        out_shape=jax.ShapeDtypeStruct((1, ROWS), f32),
        in_specs=[
            pl.BlockSpec(memory_space=pl.ANY),
            pl.BlockSpec(memory_space=pltpu.VMEM),
            pl.BlockSpec(memory_space=pl.ANY),
        ],
        out_specs=pl.BlockSpec(memory_space=pltpu.VMEM),
        scratch_shapes=[
            pltpu.VMEM((ROWS, E), bf),
            pltpu.VMEM((ROWS, E), bf),
            pltpu.VMEM((DEVICES, SLOT, E), bf),
            pltpu.VMEM((DEVICES, SLOT, E), bf),
            pltpu.VMEM((ROWS, E), bf),
            pltpu.VMEM((ROWS, E), bf),
            pltpu.VMEM((ROWS, E), bf),
            pltpu.VMEM((4, 1, ROWS), i32),
            pltpu.VMEM((4, 1, ROWS), i32),
            pltpu.VMEM((2, GROUPS, 1, PIECE), f32),
            pltpu.VMEM((3, GROUPS, 1, PIECE), f32),
            pltpu.VMEM((GROUPS, 1, PIECE), f32),
            pltpu.VMEM((DEVICES, 1, PIECE), f32),
            pltpu.VMEM((2, GROUPS, 1, PIECE), f32),
            dma((4,)),
            dma((4,)),
            dma,
            dma, dma,
            dma, dma((GROUPS,)),
            dma, dma,
            dma, dma((GROUPS,)),
            dma((2,)), dma((2,)),
            dma, dma,
        ],
        compiler_params=pltpu.CompilerParams(
            collective_id=0, has_side_effects=True, vmem_limit_bytes=48 * 2**20
        ),
        name="dedup_scores",
    )(embeddings, target.reshape(1, ROWS), cluster_labels.reshape(BLOCKS, 1, ROWS))
    return result.reshape(ROWS)


def solution(mesh):
    return jax.shard_map(
        body,
        mesh=mesh,
        in_specs=(P(("group", "block"), None), P(("group", "block")), P("group")),
        out_specs=P(("group", "block")),
        check_vma=False,
    )
```

time: 232 us -> 76.6 us (0.33)
  waiting for transfers between devices: 107 us -> 0 us
  Pallas kernels: 0 us -> 72.6 us
  blocking collectives: 66 us -> 0 us
  between operations: 12.8 us -> 0.01 us
  starting transfers between devices: 11.9 us -> 0 us
  other arithmetic: 11 us -> 0 us
  matrix products: 10.9 us -> 0 us
  local copies, waits for them, and re-layouts: 11.6 us -> 3.71 us
    ppermute x4 -> x0, waiting for transfers between devices: 107 us -> none  [passed_along(): return lax.ppermute(x, axis, pairs)]
    pallas_call x0 -> x1, Pallas kernels: none -> 72.6 us  [body(): pl.pallas_call(kernel, out_shape=jax.ShapeDtypeStruct((1, ROWS), f32), in...]
    all_to_all x2 -> x0, blocking collectives: 66 us -> none  [the longest x1 40.8 us: body(): lax.all_to_all(outgoing, ('group', 'block'), split_axis=0, concat_axis=0,...]
    ppermute x4 -> x0, starting transfers between devices: 11.9 us -> none  [passed_along(): return lax.ppermute(x, axis, pairs)]
    dot_general x3 -> x0, matrix products: 10.9 us -> none  [masked_gram(): lax.dot_general(received, piece, (((1,), (1,)), ((), ())), preferred_elem...]
    gather x1 -> x0, local copies, waits for them, and re-layouts: 8.84 us -> none  [body(): return returned[position]]
    scatter x1 -> x0, other arithmetic: 7.24 us -> none  [body(): outgoing = jnp.zeros_like(unit).at[position].set(unit)]
    unnamed x4 -> x7, local copies, waits for them, and re-layouts: 0.01 us -> 3.71 us
  transfers between devices with their start and end apart: 4 -> 0, of which waited for: 4 -> 0; matrix products, arithmetic and copies ran while one was open for 4% -> 0% of each run, Pallas kernels for 0% -> 0%
where the time goes in v2:
time: 76.6 us; the launch traced here: 76.4 us
  Pallas kernels  72.6 us (95%)
  local copies, waits for them, and re-layouts  3.71 us (5%)
    pallas_call x1, Pallas kernels, body(): pl.pallas_call(kernel, out_shape=jax.ShapeDtypeStruct((1, ROWS), f32), in...  72.6 us
    unnamed x7, local copies, waits for them, and re-layouts  3.71 us

profile of v2, /device:TPU:1, one launch (start us, length us, event | category | flops | bytes accessed | tf_op | source)
XLA Modules:
  0.0 76.4 jit_solution(13761849004478357181)
XLA Ops:
  0.0 0.0 copy-start
  0.0 1.6 %copy-done = bf16[1024,1024]{1,0:T(8,128)(2,1)S(1)} copy-done((bf16[1024,1024]{1,0:T(8,128)(2,1)S(1)}, bf16[1024,1024]{1,0:T(8,128)(2,1)}, u32[]{:S(2)}) %copy-start) | copy-done | bytes 2097176
  1.6 0.0 copy-start.1
  1.6 0.8 %copy-done.1 = s32[16384]{0:T(1024)S(1)} copy-done((s32[16384]{0:T(1024)S(1)}, s32[16384]{0:T(1024)}, u32[]{:S(2)}) %copy-start.1) | copy-done | bytes 65560
  2.4 0.0 copy-start.2
  2.4 0.7 copy-done.2
  3.1 72.6 %dedup_scores.1 = f32[1,1024]{1,0:T(1,128)S(1)} custom-call(bf16[1024,1024]{1,0:T(8,128)(2,1)S(1)} %copy-done, s32[1,1024]{1,0:T(1,128)S(1)} %bitcast.5, s32[16,1,1024]{2,1,0:T(1,128)S(1)} %bitcast.3), custom_call_target="tpu_custom_call" | custom-call | tf_op jit(solution)/shard_map/dedup_scores/pallas_call | solution.py:336
  75.8 0.6 copy.5
Async XLA Ops:
  0.0 1.6 %copy-start = (bf16[1024,1024]{1,0:T(8,128)(2,1)S(1)}, bf16[1024,1024]{1,0:T(8,128)(2,1)}, u32[]{:S(2)}) copy-start(bf16[1024,1024]{1,0:T(8,128)(2,1)} %emb.1) | copy-start | bytes 6291460
  1.6 0.8 %copy-start.1 = (s32[16384]{0:T(1024)S(1)}, s32[16384]{0:T(1024)}, u32[]{:S(2)}) copy-start(s32[16384]{0:T(1024)} %param.5) | copy-start | bytes 196612
  2.4 0.7 copy-start.2

commit v3 on v0

v3 whole, which is shorter than its diff:
```python
import jax
import jax.numpy as jnp
from jax import lax
from jax.experimental import pallas as pl
from jax.experimental.pallas import tpu as pltpu
from jax.sharding import PartitionSpec as P

MESH = pl.DeviceIdType.MESH
E = 1024
ROWS = 1024
GROUPS = 8
BLOCKS = 16
DEVICES = GROUPS * BLOCKS
SLOT = ROWS // DEVICES
LANES = 128
CHUNKS = ROWS // LANES
STAGES = 4
PIECE = ROWS // STAGES
LOW = -2.0
OWN, NEAR, SIB = 0, 1, 2
OFFSETS = (2, 1, 3, 0)


def place_of(block):
    z, y = block // 4, block % 4
    turn = z % 2
    return turn * 4 + y + turn * (3 - 2 * y)


def block_at(half, place):
    turn, r = place // 4, place % 4
    return (2 * half + turn) * 4 + r + turn * (3 - 2 * r)


def partner(block, core):
    place = place_of(block) - 1 + 2 * core
    ok = (place >= 0) & (place < 8)
    return block_at(block // 8, jnp.clip(place, 0, 7)), ok


def kernel(
    emb, tgt_hbm, lab, out,
    raw, unit, outgoing, recv, blk, tgt, lab_loc, lab_out, lab_in, lane_lab, col_lab, col_best, row_best, score, back, picks, turned,
    raw_sem, lab_sem, tgt_sem, self_sem, lab_ss, lab_rs, a2a_ss, a2a_rs, rl_ss, rl_rs, sib_ss, sib_rs,
    back_ss, back_rs,
):
    gme = lax.axis_index("group")
    bme = lax.axis_index("block")
    me = gme * BLOCKS + bme
    core = gme % 2
    gsib = gme + 1 - 2 * core
    xme, zme, yme = gme // 2, bme // 4, bme % 4
    place = place_of(bme)
    sum_me = xme + zme + yme
    half = bme // 8
    to_block, has_to = partner(bme, core)
    from_block, has_from = partner(bme, 1 - core)
    dev_sib = (gsib, bme)
    sum_from = xme + from_block // 4 + from_block % 4
    class_me = lax.rem(sum_me, 4)

    raw_copies = []
    for i in range(4):
        rows = pl.ds(i * 256, 256)
        raw_copies.append(pltpu.make_async_copy(emb.at[rows], raw.at[rows], raw_sem.at[i]))
    tgt_copy = pltpu.make_async_copy(tgt_hbm, tgt, tgt_sem)
    lab_copies = []
    for i in range(4):
        b = jnp.clip(2 * place - 1 + i, 0, BLOCKS - 1)
        lab_copies.append(pltpu.make_async_copy(lab.at[b], lab_loc.at[i], lab_sem.at[i]))
    for copy in raw_copies + [tgt_copy] + lab_copies:
        copy.start()

    barrier = pltpu.get_barrier_semaphore()

    def greet(j, _):
        peer = (me + j) % DEVICES
        pl.semaphore_signal(
            barrier, inc=1, device_id=(peer // BLOCKS, peer % BLOCKS), device_id_type=MESH
        )
        return 0

    lax.fori_loop(1, DEVICES, greet, 0, unroll=False)

    for which in range(3):
        col_best[which] = jnp.full((8, ROWS), LOW, jnp.float32)
        for t in range(CHUNKS):
            row_best[which, t] = jnp.full((1, LANES), LOW, jnp.float32)
            col_lab[which, t] = jnp.full((1, LANES), -1.0, jnp.float32)

    for i in range(4):
        raw_copies[i].wait()
        for j in range(2):
            rows = pl.ds(i * 256 + j * 128, 128)
            values = raw[rows, :].astype(jnp.float32)
            squares = jnp.sum(values * values, axis=1, keepdims=True)
            unit[rows, :] = (values * lax.rsqrt(squares + 1e-06)).astype(jnp.bfloat16)

    tgt_copy.wait()
    target = tgt[...]
    row_block = target // ROWS
    t_core = row_block % 2
    t_group = row_block // (2 * BLOCKS) * 2 + t_core
    t_half = row_block // BLOCKS % 2
    t_place = row_block % BLOCKS // 2
    home = t_group * BLOCKS + block_at(t_half, t_place)
    slot_of = target % SLOT
    position = home * SLOT + slot_of
    row_iota = lax.broadcasted_iota(jnp.int32, (LANES, ROWS), 0)

    def permute(q, _):
        piece = (gme + q) % GROUPS
        onehot = jnp.where(row_iota == position - piece * LANES, 1.0, 0.0).astype(jnp.bfloat16)
        picked = jnp.dot(onehot, unit[...], preferred_element_type=jnp.float32)
        outgoing[pl.ds(piece * BLOCKS, BLOCKS)] = picked.reshape(BLOCKS, SLOT, E).astype(jnp.bfloat16)
        return 0

    lax.fori_loop(0, GROUPS, permute, 0, unroll=False)
    t_to, t_ok = partner(home % BLOCKS, t_core)
    dev_iota = lax.broadcasted_iota(jnp.int32, (DEVICES, ROWS), 0)
    devs = (home, t_group * BLOCKS + t_to, home + (1 - 2 * t_core) * BLOCKS)
    for which in range(3):
        picks[which] = jnp.where(dev_iota == devs[which], 1.0, 0.0).astype(jnp.bfloat16)

    for copy in lab_copies:
        copy.wait()
    stored = lax.broadcasted_iota(jnp.int32, (1, ROWS), 1)
    slot_no = stored // SLOT
    s_class, s_block, s_core = slot_no // 32, slot_no % 32 // 2, slot_no % 2
    s_x = (s_class - s_block // 4 - s_block % 4 + 8) % 4
    natural = ((2 * s_x + s_core) * BLOCKS + s_block) * SLOT + stored % SLOT
    lab_all = jnp.concatenate([lab_loc[i] for i in range(4)], axis=0)
    high = lab_all // 256
    halves = jnp.concatenate([high, lab_all - 256 * high], axis=0).astype(jnp.float32).astype(jnp.bfloat16)
    moved = jnp.zeros((8, ROWS), jnp.float32)
    for t in range(CHUNKS):
        move = jnp.where(row_iota == natural - t * LANES, 1.0, 0.0).astype(jnp.bfloat16)
        moved = moved + jnp.dot(
            halves[:, t * LANES : (t + 1) * LANES], move, preferred_element_type=jnp.float32
        )
    lab_new = moved[:4] * 256.0 + moved[4:]
    for i in range(4):
        lab_out[i] = lab_new[i : i + 1]

    pl.semaphore_wait(barrier, DEVICES - 1)

    lab_copy = pltpu.make_async_remote_copy(
        lab_out, lab_in, lab_ss, lab_rs, device_id=dev_sib, device_id_type=MESH
    )
    lab_copy.start()
    pltpu.make_async_copy(outgoing.at[me], recv.at[OWN, class_me, zme, yme, core], a2a_rs.at[OWN, 0]).start()

    @pl.when(has_from)
    def _():
        pltpu.make_async_copy(
            outgoing.at[gme * BLOCKS + from_block],
            recv.at[NEAR, class_me, zme, yme, core],
            a2a_rs.at[NEAR, 2 * lax.rem(sum_from - sum_me + 4, 4)],
        ).start()

    routes = []
    for c in range(2):
        to_core = lax.rem(core + c, 2)
        sign = 2 * to_core - 1
        for dz in OFFSETS:
            for dy in OFFSETS:
                z, y = lax.rem(zme + dz, 4), lax.rem(yme + dy, 4)
                turn = lax.rem(z, 2)
                along = 1 - 2 * turn
                way = sign * along
                on_y = (y + way >= 0) & (y + way <= 3)
                on_z = (y == 3) & (way == 1)
                far_y = {0: way == 0, 1: way == -1, 2: way != 0, 3: way == 1}[dy]
                far_z = {0: turn == 2, 1: turn == 1, 2: turn != 2, 3: turn == 0}[dz]
                second = (on_y & far_y) | (on_z & far_z)
                block = z * 4 + y
                other = jnp.where(on_y, block + way, block + 4 * along)
                routes.append((c, 8 - dz - dy, block, jnp.where(second, NEAR, OWN), jnp.where(second, other, block)))

    def send_stage(q, _):
        for c, dx, home_block, which, block in routes:
            to_group = 2 * lax.rem(xme + q + dx, 4) + (core if c == 0 else 1 - core)

            def send():
                pltpu.make_async_remote_copy(
                    outgoing.at[to_group * BLOCKS + home_block],
                    recv.at[which, class_me, zme, yme, core],
                    a2a_ss,
                    a2a_rs.at[which, 2 * q + c],
                    device_id=(to_group, block),
                    device_id_type=MESH,
                ).start()

            if c == 0:
                pl.when((to_group != gme) | (block != bme))(send)
            else:
                send()
        return 0

    lax.fori_loop(0, STAGES, send_stage, 0, unroll=False)

    lab_copy.wait()
    labels = [
        jnp.where(half == core, lab_out[i], lab_in[i]) for i in range(4)
    ]
    is0 = core == 0
    sides = [
        jnp.where(is0, labels[1], labels[2]),
        jnp.where(has_from, jnp.where(is0, labels[3], labels[0]), -2.0),
        jnp.where(is0, labels[2], labels[1]),
    ]
    for which in range(3):
        for t in range(CHUNKS):
            lane_lab[which, t] = sides[which][:, t * LANES : (t + 1) * LANES]

    eight = recv.at[OWN, 0, 0]
    sixteen = recv.at[OWN, 0, pl.ds(0, 2)]
    thirty_two = recv.at[OWN, 0]

    def await_bytes(ref, sem):
        pltpu.make_async_copy(ref, ref, sem).wait()

    def hand_on(which, n, a, c, dy, dz, block):
        for step in range(2):
            yy = lax.rem(yme + step * dy + 4, 4)
            zz = lax.rem(zme + step * dz + 4, 4)

            def go(src, dst):
                pltpu.make_async_remote_copy(
                    src, dst, rl_ss.at[which], rl_rs.at[1 - which, n], device_id=(gme, block), device_id_type=MESH
                ).start()

            @pl.when(dy != 0)
            def _():
                go(recv.at[which, a, :, yy, c], recv.at[1 - which, a, :, yy, c])

            @pl.when(dy == 0)
            def _():
                go(recv.at[which, a, zz, :, c], recv.at[1 - which, a, zz, :, c])

    def own_class(q):
        return lax.rem(sum_me - q + 4, 4)

    def near_class(q):
        return lax.rem(sum_from - q + 4, 4)

    def first(q, c):
        n = 2 * q + c
        from_core = lax.rem(core + c, 2)

        @pl.when(has_to)
        def _():
            await_bytes(eight, a2a_rs.at[OWN, n])
            hand_on(OWN, n, own_class(q), from_core, yme - to_block % 4, zme - to_block // 4, to_block)

        @pl.when(jnp.logical_not(has_to))
        def _():
            await_bytes(sixteen, a2a_rs.at[OWN, n])

        @pl.when(has_from)
        def _():
            await_bytes(eight, a2a_rs.at[NEAR, n])
            hand_on(NEAR, n, near_class(q), from_core, yme - from_block % 4, zme - from_block // 4, from_block)

    def lay_out(which, x):
        got = recv[which, x].astype(jnp.float32)
        blk[which, pl.ds(x * PIECE, PIECE), :] = got.reshape(PIECE, E).astype(jnp.bfloat16)
        for c in range(2):
            col_lab[which, 2 * x + c] = lane_lab[which, 2 * x + c]

    r_iota = lax.broadcasted_iota(jnp.int32, (PIECE, LANES), 0)
    c_iota = lax.broadcasted_iota(jnp.int32, (PIECE, LANES), 1)
    ahead = r_iota - c_iota

    def product(a, x, b, same_block=False):
        gram = lax.dot_general(
            blk[a, pl.ds(x * PIECE, PIECE), :],
            blk[b],
            (((1,), (1,)), ((), ())),
            preferred_element_type=jnp.float32,
        )
        a_lab = jnp.concatenate(
            [jnp.broadcast_to(lane_lab[a, 2 * x + c], (LANES, LANES)).T for c in range(2)], axis=0
        )
        rows_best = jnp.full((PIECE, LANES), LOW, jnp.float32)
        for t in range(CHUNKS):
            cut = slice(t * LANES, (t + 1) * LANES)
            same = a_lab == col_lab[b, t]
            if same_block:
                same = same & (ahead != t * LANES - x * PIECE)
            masked = jnp.where(same, gram[:, cut], LOW)
            rows_best = jnp.maximum(rows_best, masked)
            col_best[b, :, cut] = jnp.maximum(
                col_best[b, :, cut], jnp.max(masked.reshape(PIECE // 8, 8, LANES), axis=0)
            )
        return rows_best

    def fold_rows(which, x, rows_best):
        for c in range(2):
            line = jnp.max(rows_best[c * LANES : (c + 1) * LANES].T, axis=0, keepdims=True)
            row_best[which, 2 * x + c] = jnp.maximum(row_best[which, 2 * x + c], line)

    def complete(q):
        x, w = own_class(q), near_class(q)

        @pl.when(has_to)
        def _():
            for c in range(2):
                await_bytes(eight, rl_rs.at[OWN, 2 * q + c])

        pltpu.make_async_remote_copy(
            recv.at[OWN, x], recv.at[SIB, x], sib_ss, sib_rs.at[q], device_id=dev_sib, device_id_type=MESH
        ).start()
        lay_out(OWN, x)

        @pl.when(has_from)
        def _():
            for c in range(2):
                await_bytes(eight, rl_rs.at[NEAR, 2 * q + c])
            lay_out(NEAR, w)

        own_rows = product(OWN, x, OWN, same_block=True)
        fold_rows(OWN, x, jnp.maximum(own_rows, product(OWN, x, NEAR)))
        fold_rows(NEAR, w, product(NEAR, w, OWN))

    third = 1 - core

    def sibling(q):
        x, w = own_class(q), near_class(q)
        await_bytes(thirty_two, sib_rs.at[q])
        lay_out(SIB, x)
        fold_rows(SIB, x, product(SIB, x, third))
        v = jnp.where(core == 0, w, x)
        fold_rows(third, v, product(third, v, SIB))

    def step(s, _):
        @pl.when(s < STAGES)
        def _():
            first(s, 0)
            first(s, 1)

        @pl.when((s >= 1) & (s < STAGES + 1))
        def _():
            complete(s - 1)

        @pl.when(s >= 2)
        def _():
            sibling(s - 2)

        return 0

    lax.fori_loop(0, STAGES + 2, step, 0, unroll=False)

    for which in range(3):
        for t in range(CHUNKS):
            cut = slice(t * LANES, (t + 1) * LANES)
            line = jnp.max(col_best[which, :, cut], axis=0, keepdims=True)
            score[which, t] = jnp.maximum(line, row_best[which, t])

    own_back = pltpu.make_async_copy(score.at[:, 2 * class_me + zme // 2], back.at[me], self_sem)
    own_back.start()

    near_coords = [(lax.rem(zme + dz, 4), lax.rem(yme + dy, 4)) for dz in OFFSETS for dy in OFFSETS]

    def give(i, _):
        group = lax.rem(gme + 4 + i, GROUPS)
        for n, (z, y) in enumerate(near_coords):
            chunk = 2 * lax.rem(group // 2 + z + y, 4) + z // 2

            def send():
                pltpu.make_async_remote_copy(
                    score.at[:, chunk],
                    back.at[me],
                    back_ss,
                    back_rs,
                    device_id=(group, z * 4 + y),
                    device_id_type=MESH,
                ).start()

            if n == BLOCKS - 1:
                pl.when(i != 4)(send)
            else:
                send()
        return 0

    lax.fori_loop(0, GROUPS, give, 0, unroll=False)

    await_bytes(outgoing.at[pl.ds(0, DEVICES - 2)], a2a_ss)

    @pl.when(jnp.logical_not(has_from))
    def _():
        await_bytes(outgoing.at[0], a2a_ss)

    @pl.when(has_to)
    def _():
        await_bytes(recv.at[OWN, pl.ds(0, 2)], rl_ss.at[OWN])

    @pl.when(has_from)
    def _():
        await_bytes(recv.at[OWN, pl.ds(0, 2)], rl_ss.at[NEAR])

    await_bytes(recv.at[OWN], sib_ss)
    own_back.wait()
    part = back.at[pl.ds(0, DEVICES - 1)]
    await_bytes(part, back_ss)
    await_bytes(part, back_rs)

    slot_iota = lax.broadcasted_iota(jnp.int32, (SLOT, ROWS), 0)
    best = jnp.full((SLOT, ROWS), LOW, jnp.float32)
    for which in range(3):
        turned[...] = back[:, which, 0, :].T
        rest = turned[pl.ds((lax.rem(bme, 8) * 2 + core) * SLOT, SLOT), :]
        parts = []
        for _ in range(3):
            parts.append(rest.astype(jnp.bfloat16))
            rest = rest - parts[-1].astype(jnp.float32)
        slots = jnp.zeros((SLOT, ROWS), jnp.float32)
        for part in parts:
            slots = slots + jnp.dot(part, picks[which], preferred_element_type=jnp.float32)
        if which == NEAR:
            slots = jnp.where(t_ok, slots, LOW)
        best = jnp.maximum(best, slots)
    out[...] = jnp.sum(jnp.where(slot_iota == slot_of, best, 0.0), axis=0, keepdims=True)


def body(embeddings, target, cluster_labels):
    bf, f32, i32 = jnp.bfloat16, jnp.float32, jnp.int32
    dma = pltpu.SemaphoreType.DMA
    result = pl.pallas_call(
        kernel,
        out_shape=jax.ShapeDtypeStruct((1, ROWS), f32),
        in_specs=[pl.BlockSpec(memory_space=pl.ANY)] * 3,
        out_specs=pl.BlockSpec(memory_space=pltpu.VMEM),
        scratch_shapes=[
            pltpu.VMEM((ROWS, E), bf),
            pltpu.VMEM((ROWS, E), bf),
            pltpu.VMEM((DEVICES, SLOT, E), bf),
            pltpu.VMEM((3, 4, 4, 4, 2, SLOT, E), bf),
            pltpu.VMEM((3, ROWS, E), bf),
            pltpu.VMEM((1, ROWS), i32),
            pltpu.VMEM((4, 1, ROWS), i32),
            pltpu.VMEM((4, 1, ROWS), f32),
            pltpu.VMEM((4, 1, ROWS), f32),
            pltpu.VMEM((3, CHUNKS, 1, LANES), f32),
            pltpu.VMEM((3, CHUNKS, 1, LANES), f32),
            pltpu.VMEM((3, 8, ROWS), f32),
            pltpu.VMEM((3, CHUNKS, 1, LANES), f32),
            pltpu.VMEM((3, CHUNKS, 1, LANES), f32),
            pltpu.VMEM((DEVICES, 3, 1, LANES), f32),
            pltpu.VMEM((3, DEVICES, ROWS), bf),
            pltpu.VMEM((LANES, DEVICES), f32),
            dma((4,)),
            dma((4,)),
            dma,
            dma,
            dma, dma,
            dma, dma((2, GROUPS)),
            dma((2,)), dma((2, GROUPS)),
            dma, dma((STAGES,)),
            dma, dma,
        ],
        compiler_params=pltpu.CompilerParams(
            collective_id=0, has_side_effects=True, vmem_limit_bytes=60 * 2**20
        ),
        name="dedup_scores",
    )(embeddings, target.reshape(1, ROWS), cluster_labels.reshape(BLOCKS, 1, ROWS))
    return result.reshape(ROWS)


def solution(mesh):
    return jax.shard_map(
        body,
        mesh=mesh,
        in_specs=(P(("group", "block"), None), P(("group", "block")), P("group")),
        out_specs=P(("group", "block")),
        check_vma=False,
    )
```

time: 232 us -> 69.4 us (0.30)
  waiting for transfers between devices: 107 us -> 0 us
  Pallas kernels: 0 us -> 68 us
  blocking collectives: 66 us -> 0 us
  between operations: 12.8 us -> 0.01 us
  starting transfers between devices: 11.9 us -> 0 us
  other arithmetic: 11 us -> 0 us
  matrix products: 10.9 us -> 0 us
  local copies, waits for them, and re-layouts: 11.6 us -> 1.28 us
    ppermute x4 -> x0, waiting for transfers between devices: 107 us -> none  [passed_along(): return lax.ppermute(x, axis, pairs)]
    pallas_call x0 -> x1, Pallas kernels: none -> 68 us  [body(): pl.pallas_call(kernel, out_shape=jax.ShapeDtypeStruct((1, ROWS), f32), in...]
    all_to_all x2 -> x0, blocking collectives: 66 us -> none  [the longest x1 40.8 us: body(): lax.all_to_all(outgoing, ('group', 'block'), split_axis=0, concat_axis=0,...]
    ppermute x4 -> x0, starting transfers between devices: 11.9 us -> none  [passed_along(): return lax.ppermute(x, axis, pairs)]
    dot_general x3 -> x0, matrix products: 10.9 us -> none  [masked_gram(): lax.dot_general(received, piece, (((1,), (1,)), ((), ())), preferred_elem...]
    gather x1 -> x0, local copies, waits for them, and re-layouts: 8.84 us -> none  [body(): return returned[position]]
    scatter x1 -> x0, other arithmetic: 7.24 us -> none  [body(): outgoing = jnp.zeros_like(unit).at[position].set(unit)]
  transfers between devices with their start and end apart: 4 -> 0, of which waited for: 4 -> 0; matrix products, arithmetic and copies ran while one was open for 4% -> 0% of each run, Pallas kernels for 0% -> 0%
where the time goes in v3:
time: 69.4 us; the launch traced here: 69.3 us
  Pallas kernels  68 us (98%)
  local copies, waits for them, and re-layouts  1.28 us (2%)
    pallas_call x1, Pallas kernels, body(): pl.pallas_call(kernel, out_shape=jax.ShapeDtypeStruct((1, ROWS), f32), in...  68 us

profile of v3, /device:TPU:1, one launch (start us, length us, event | category | flops | bytes accessed | tf_op | source)
XLA Modules:
  0.0 69.3 jit_solution(15102963130063061699)
XLA Ops:
  0.0 68.0 %dedup_scores.1 = f32[1,1024]{1,0:T(1,128)} custom-call(bf16[1024,1024]{1,0:T(8,128)(2,1)} %emb.1, s32[1,1024]{1,0:T(1,128)} %bitcast.5, s32[16,1,1024]{2,1,0:T(1,128)} %bitcast.3), custom_call_target="tpu_custom_call" | custom-call | tf_op jit(solution)/shard_map/dedup_scores/pallas_call | solution.py:429
  68.0 1.3 %copy.5 = f32[1024]{0:T(1024)} copy(f32[1024]{0:T(1024)} %bitcast.4) | data formatting | bytes 8192

commit v4 on v3

--- a/solution.py
+++ b/solution.py
@@ -42,7 +42,7 @@
     emb, tgt_hbm, lab, out,
     raw, unit, outgoing, recv, blk, tgt, lab_loc, lab_out, lab_in, lane_lab, col_lab, col_best, row_best, score, back, picks, turned,
     raw_sem, lab_sem, tgt_sem, self_sem, lab_ss, lab_rs, a2a_ss, a2a_rs, rl_ss, rl_rs, sib_ss, sib_rs,
-    back_ss, back_rs,
+    back_ss, back_rs, row_sem,
 ):
     gme = lax.axis_index("group")
     bme = lax.axis_index("block")
@@ -73,14 +73,12 @@
 
     barrier = pltpu.get_barrier_semaphore()
 
-    def greet(j, _):
-        peer = (me + j) % DEVICES
-        pl.semaphore_signal(
-            barrier, inc=1, device_id=(peer // BLOCKS, peer % BLOCKS), device_id_type=MESH
-        )
-        return 0
-
-    lax.fori_loop(1, DEVICES, greet, 0, unroll=False)
+    row = [lax.rem(bme + i, BLOCKS) for i in range(1, BLOCKS)]
+    column = [lax.rem(gme + i, GROUPS) for i in range(1, GROUPS)]
+    for block in row:
+        pl.semaphore_signal(barrier, inc=1, device_id=(gme, block), device_id_type=MESH)
+    for group in column:
+        pl.semaphore_signal(barrier, inc=1, device_id=(group, bme), device_id_type=MESH)
 
     for which in range(3):
         col_best[which] = jnp.full((8, ROWS), LOW, jnp.float32)
@@ -142,7 +140,9 @@
     for i in range(4):
         lab_out[i] = lab_new[i : i + 1]
 
-    pl.semaphore_wait(barrier, DEVICES - 1)
+    pl.semaphore_wait(barrier, len(row) + len(column))
+    for block in row:
+        pl.semaphore_signal(row_sem, inc=1, device_id=(gme, block), device_id_type=MESH)
 
     lab_copy = pltpu.make_async_remote_copy(
         lab_out, lab_in, lab_ss, lab_rs, device_id=dev_sib, device_id_type=MESH
@@ -175,26 +175,45 @@
                 second = (on_y & far_y) | (on_z & far_z)
                 block = z * 4 + y
                 other = jnp.where(on_y, block + way, block + 4 * along)
-                routes.append((c, 8 - dz - dy, block, jnp.where(second, NEAR, OWN), jnp.where(second, other, block)))
+                routes.append((c, dz, dy, block, jnp.where(second, NEAR, OWN), jnp.where(second, other, block)))
+
+    def send(q, c, x, home_block, which, block):
+        to_group = 2 * x + (core if c == 0 else 1 - core)
+        pltpu.make_async_remote_copy(
+            outgoing.at[to_group * BLOCKS + home_block],
+            recv.at[which, class_me, zme, yme, core],
+            a2a_ss,
+            a2a_rs.at[which, 2 * q + c],
+            device_id=(to_group, block),
+            device_id_type=MESH,
+        ).start()
+
+    for c, dz, dy, home_block, which, block in routes:
+        if dz == 0 and dy == 0:
+            for dx in OFFSETS:
+                if dx or c:
+                    send(dx, c, lax.rem(xme + dx, 4), home_block, which, block)
+        elif c == 0:
+
+            @pl.when(block != bme)
+            def _():
+                send((dz + dy) % 4, c, xme, home_block, which, block)
+
+    pl.semaphore_wait(row_sem, len(row))
 
     def send_stage(q, _):
-        for c, dx, home_block, which, block in routes:
-            to_group = 2 * lax.rem(xme + q + dx, 4) + (core if c == 0 else 1 - core)
-
-            def send():
-                pltpu.make_async_remote_copy(
-                    outgoing.at[to_group * BLOCKS + home_block],
-                    recv.at[which, class_me, zme, yme, core],
-                    a2a_ss,
-                    a2a_rs.at[which, 2 * q + c],
-                    device_id=(to_group, block),
-                    device_id_type=MESH,
-                ).start()
+        for c, dz, dy, home_block, which, block in routes:
+            if dz == 0 and dy == 0:
+                continue
+            dx = lax.rem(q + 8 - dz - dy, 4)
+
+            def go():
+                send(q, c, lax.rem(xme + dx, 4), home_block, which, block)
 
             if c == 0:
-                pl.when((to_group != gme) | (block != bme))(send)
+                pl.when(dx != 0)(go)
             else:
-                send()
+                go()
         return 0
 
     lax.fori_loop(0, STAGES, send_stage, 0, unroll=False)
@@ -339,13 +358,13 @@
             first(s, 0)
             first(s, 1)
 
+        @pl.when(s >= 2)
+        def _():
+            sibling(s - 2)
+
         @pl.when((s >= 1) & (s < STAGES + 1))
         def _():
             complete(s - 1)
-
-        @pl.when(s >= 2)
-        def _():
-            sibling(s - 2)
 
         return 0
 
@@ -458,6 +477,7 @@
             dma((2,)), dma((2, GROUPS)),
             dma, dma((STAGES,)),
             dma, dma,
+            pltpu.SemaphoreType.REGULAR,
         ],
         compiler_params=pltpu.CompilerParams(
             collective_id=0, has_side_effects=True, vmem_limit_bytes=60 * 2**20

time: 69.4 us -> 65.7 us (0.947)
  Pallas kernels: 68 us -> 64.3 us
    pallas_call x1, Pallas kernels: 68 us -> 64.3 us  [body(): pl.pallas_call(kernel, out_shape=jax.ShapeDtypeStruct((1, ROWS), f32), in...]
where the time goes in v4:
time: 65.7 us; the launch traced here: 65.6 us
  Pallas kernels  64.3 us (98%)
  local copies, waits for them, and re-layouts  1.28 us (2%)
    pallas_call x1, Pallas kernels, body(): pl.pallas_call(kernel, out_shape=jax.ShapeDtypeStruct((1, ROWS), f32), in...  64.3 us

profile of v4, /device:TPU:1, one launch (start us, length us, event | category | flops | bytes accessed | tf_op | source)
XLA Modules:
  0.0 65.6 jit_solution(2657789229256096107)
XLA Ops:
  0.0 64.3 %dedup_scores.1 = f32[1,1024]{1,0:T(1,128)} custom-call(bf16[1024,1024]{1,0:T(8,128)(2,1)} %emb.1, s32[1,1024]{1,0:T(1,128)} %bitcast.5, s32[16,1,1024]{2,1,0:T(1,128)} %bitcast.3), custom_call_target="tpu_custom_call" | custom-call | tf_op jit(solution)/shard_map/dedup_scores/pallas_call | solution.py:448
  64.3 1.3 %copy.5 = f32[1024]{0:T(1024)} copy(f32[1024]{0:T(1024)} %bitcast.4) | data formatting | bytes 8192

commit v5 on v4

--- a/solution.py
+++ b/solution.py
@@ -103,60 +103,17 @@
     t_place = row_block % BLOCKS // 2
     home = t_group * BLOCKS + block_at(t_half, t_place)
     slot_of = target % SLOT
-    position = home * SLOT + slot_of
-    row_iota = lax.broadcasted_iota(jnp.int32, (LANES, ROWS), 0)
-
-    def permute(q, _):
-        piece = (gme + q) % GROUPS
-        onehot = jnp.where(row_iota == position - piece * LANES, 1.0, 0.0).astype(jnp.bfloat16)
+    t_block = home % BLOCKS
+    t_class = (t_group // 2 + t_block // 4 + t_block % 4) % 4
+    position = (t_class * 32 + t_block * 2 + t_core) * SLOT + slot_of
+    row_iota = lax.broadcasted_iota(jnp.int32, (PIECE, ROWS), 0)
+
+    def permute(q):
+        a = lax.rem(class_me + q, 4)
+        onehot = jnp.where(row_iota == position - a * PIECE, 1.0, 0.0).astype(jnp.bfloat16)
         picked = jnp.dot(onehot, unit[...], preferred_element_type=jnp.float32)
-        outgoing[pl.ds(piece * BLOCKS, BLOCKS)] = picked.reshape(BLOCKS, SLOT, E).astype(jnp.bfloat16)
-        return 0
-
-    lax.fori_loop(0, GROUPS, permute, 0, unroll=False)
-    t_to, t_ok = partner(home % BLOCKS, t_core)
-    dev_iota = lax.broadcasted_iota(jnp.int32, (DEVICES, ROWS), 0)
-    devs = (home, t_group * BLOCKS + t_to, home + (1 - 2 * t_core) * BLOCKS)
-    for which in range(3):
-        picks[which] = jnp.where(dev_iota == devs[which], 1.0, 0.0).astype(jnp.bfloat16)
-
-    for copy in lab_copies:
-        copy.wait()
-    stored = lax.broadcasted_iota(jnp.int32, (1, ROWS), 1)
-    slot_no = stored // SLOT
-    s_class, s_block, s_core = slot_no // 32, slot_no % 32 // 2, slot_no % 2
-    s_x = (s_class - s_block // 4 - s_block % 4 + 8) % 4
-    natural = ((2 * s_x + s_core) * BLOCKS + s_block) * SLOT + stored % SLOT
-    lab_all = jnp.concatenate([lab_loc[i] for i in range(4)], axis=0)
-    high = lab_all // 256
-    halves = jnp.concatenate([high, lab_all - 256 * high], axis=0).astype(jnp.float32).astype(jnp.bfloat16)
-    moved = jnp.zeros((8, ROWS), jnp.float32)
-    for t in range(CHUNKS):
-        move = jnp.where(row_iota == natural - t * LANES, 1.0, 0.0).astype(jnp.bfloat16)
-        moved = moved + jnp.dot(
-            halves[:, t * LANES : (t + 1) * LANES], move, preferred_element_type=jnp.float32
-        )
-    lab_new = moved[:4] * 256.0 + moved[4:]
-    for i in range(4):
-        lab_out[i] = lab_new[i : i + 1]
-
-    pl.semaphore_wait(barrier, len(row) + len(column))
-    for block in row:
-        pl.semaphore_signal(row_sem, inc=1, device_id=(gme, block), device_id_type=MESH)
-
-    lab_copy = pltpu.make_async_remote_copy(
-        lab_out, lab_in, lab_ss, lab_rs, device_id=dev_sib, device_id_type=MESH
-    )
-    lab_copy.start()
-    pltpu.make_async_copy(outgoing.at[me], recv.at[OWN, class_me, zme, yme, core], a2a_rs.at[OWN, 0]).start()
-
-    @pl.when(has_from)
-    def _():
-        pltpu.make_async_copy(
-            outgoing.at[gme * BLOCKS + from_block],
-            recv.at[NEAR, class_me, zme, yme, core],
-            a2a_rs.at[NEAR, 2 * lax.rem(sum_from - sum_me + 4, 4)],
-        ).start()
+        slots = PIECE // SLOT
+        outgoing[pl.ds(a * slots, slots)] = picked.reshape(slots, SLOT, E).astype(jnp.bfloat16)
 
     routes = []
     for c in range(2):
@@ -178,30 +135,29 @@
                 routes.append((c, dz, dy, block, jnp.where(second, NEAR, OWN), jnp.where(second, other, block)))
 
     def send(q, c, x, home_block, which, block):
-        to_group = 2 * x + (core if c == 0 else 1 - core)
+        to_core = core if c == 0 else 1 - core
         pltpu.make_async_remote_copy(
-            outgoing.at[to_group * BLOCKS + home_block],
+            outgoing.at[lax.rem(class_me + q, 4) * 32 + home_block * 2 + to_core],
             recv.at[which, class_me, zme, yme, core],
             a2a_ss,
             a2a_rs.at[which, 2 * q + c],
-            device_id=(to_group, block),
+            device_id=(2 * x + to_core, block),
             device_id_type=MESH,
         ).start()
 
-    for c, dz, dy, home_block, which, block in routes:
-        if dz == 0 and dy == 0:
-            for dx in OFFSETS:
+    def send_known(q):
+        for c, dz, dy, home_block, which, block in routes:
+            dx = (q - dz - dy) % 4
+            if dz == 0 and dy == 0:
                 if dx or c:
-                    send(dx, c, lax.rem(xme + dx, 4), home_block, which, block)
-        elif c == 0:
-
-            @pl.when(block != bme)
-            def _():
-                send((dz + dy) % 4, c, xme, home_block, which, block)
-
-    pl.semaphore_wait(row_sem, len(row))
-
-    def send_stage(q, _):
+                    send(q, c, lax.rem(xme + dx, 4), home_block, which, block)
+            elif c == 0 and dx == 0:
+
+                @pl.when(block != bme)
+                def _():
+                    send(q, c, xme, home_block, which, block)
+
+    def send_rest(q, _):
         for c, dz, dy, home_block, which, block in routes:
             if dz == 0 and dy == 0:
                 continue
@@ -216,7 +172,73 @@
                 go()
         return 0
 
-    lax.fori_loop(0, STAGES, send_stage, 0, unroll=False)
+    def send_all(q, _):
+        permute(q)
+        for c, dz, dy, home_block, which, block in routes:
+            dx = lax.rem(q + 8 - dz - dy, 4)
+
+            def go():
+                send(q, c, lax.rem(xme + dx, 4), home_block, which, block)
+
+            if c == 0 and (dz or dy):
+                pl.when((dx != 0) | (block != bme))(go)
+            else:
+                go()
+        return 0
+
+    permute(0)
+    pl.semaphore_wait(barrier, len(row) + len(column))
+    for block in row:
+        pl.semaphore_signal(row_sem, inc=1, device_id=(gme, block), device_id_type=MESH)
+    send_known(0)
+    pltpu.make_async_copy(
+        outgoing.at[class_me * 32 + bme * 2 + core],
+        recv.at[OWN, class_me, zme, yme, core],
+        a2a_rs.at[OWN, 0],
+    ).start()
+    permute(1)
+    send_known(1)
+    pl.semaphore_wait(row_sem, len(row))
+    lax.fori_loop(0, 2, send_rest, 0, unroll=False)
+    lax.fori_loop(2, STAGES, send_all, 0, unroll=False)
+
+    @pl.when(has_from)
+    def _():
+        pltpu.make_async_copy(
+            outgoing.at[lax.rem(sum_from, 4) * 32 + from_block * 2 + core],
+            recv.at[NEAR, class_me, zme, yme, core],
+            a2a_rs.at[NEAR, 2 * lax.rem(sum_from - sum_me + 4, 4)],
+        ).start()
+
+    for copy in lab_copies:
+        copy.wait()
+    stored = lax.broadcasted_iota(jnp.int32, (1, ROWS), 1)
+    slot_no = stored // SLOT
+    s_class, s_block, s_core = slot_no // 32, slot_no % 32 // 2, slot_no % 2
+    s_x = (s_class - s_block // 4 - s_block % 4 + 8) % 4
+    natural = ((2 * s_x + s_core) * BLOCKS + s_block) * SLOT + stored % SLOT
+    lab_all = jnp.concatenate([lab_loc[i] for i in range(4)], axis=0)
+    high = lab_all // 256
+    halves = jnp.concatenate([high, lab_all - 256 * high], axis=0).astype(jnp.float32).astype(jnp.bfloat16)
+    moved = jnp.zeros((8, ROWS), jnp.float32)
+    for t in range(CHUNKS):
+        move = jnp.where(row_iota[:LANES] == natural - t * LANES, 1.0, 0.0).astype(jnp.bfloat16)
+        moved = moved + jnp.dot(
+            halves[:, t * LANES : (t + 1) * LANES], move, preferred_element_type=jnp.float32
+        )
+    lab_new = moved[:4] * 256.0 + moved[4:]
+    for i in range(4):
+        lab_out[i] = lab_new[i : i + 1]
+
+    lab_copy = pltpu.make_async_remote_copy(
+        lab_out, lab_in, lab_ss, lab_rs, device_id=dev_sib, device_id_type=MESH
+    )
+    lab_copy.start()
+    t_to, t_ok = partner(home % BLOCKS, t_core)
+    dev_iota = lax.broadcasted_iota(jnp.int32, (DEVICES, ROWS), 0)
+    devs = (home, t_group * BLOCKS + t_to, home + (1 - 2 * t_core) * BLOCKS)
+    for which in range(3):
+        picks[which] = jnp.where(dev_iota == devs[which], 1.0, 0.0).astype(jnp.bfloat16)
 
     lab_copy.wait()
     labels = [
@@ -370,13 +392,25 @@
 
     lax.fori_loop(0, STAGES + 2, step, 0, unroll=False)
 
+    lines = []
     for which in range(3):
+        cols = [
+            jnp.max(col_best[which, :, t * LANES : (t + 1) * LANES], axis=0, keepdims=True)
+            for t in range(CHUNKS)
+        ]
+        lines.append(jnp.maximum(jnp.concatenate(cols, axis=0), row_best[which][:, 0, :]))
+    lane = lax.broadcasted_iota(jnp.int32, (CHUNKS, LANES), 1)
+    for j in range(LANES // 16):
+        own, near, sib = (
+            pltpu.roll(line, (16 * which - 16 * j) % LANES, 1) for which, line in enumerate(lines)
+        )
+        packed = jnp.where(lane < 16, own, jnp.where(lane < 32, near, sib))
         for t in range(CHUNKS):
-            cut = slice(t * LANES, (t + 1) * LANES)
-            line = jnp.max(col_best[which, :, cut], axis=0, keepdims=True)
-            score[which, t] = jnp.maximum(line, row_best[which, t])
-
-    own_back = pltpu.make_async_copy(score.at[:, 2 * class_me + zme // 2], back.at[me], self_sem)
+            score[j, t] = packed[t : t + 1]
+
+    own_back = pltpu.make_async_copy(
+        score.at[lax.rem(bme, 8), 2 * class_me + zme // 2], back.at[me], self_sem
+    )
     own_back.start()
 
     near_coords = [(lax.rem(zme + dz, 4), lax.rem(yme + dy, 4)) for dz in OFFSETS for dy in OFFSETS]
@@ -388,7 +422,7 @@
 
             def send():
                 pltpu.make_async_remote_copy(
-                    score.at[:, chunk],
+                    score.at[lax.rem(z, 2) * 4 + y, chunk],
                     back.at[me],
                     back_ss,
                     back_rs,
@@ -426,9 +460,9 @@
 
     slot_iota = lax.broadcasted_iota(jnp.int32, (SLOT, ROWS), 0)
     best = jnp.full((SLOT, ROWS), LOW, jnp.float32)
+    turned[...] = back[:, 0, :].T
     for which in range(3):
-        turned[...] = back[:, which, 0, :].T
-        rest = turned[pl.ds((lax.rem(bme, 8) * 2 + core) * SLOT, SLOT), :]
+        rest = turned[pl.ds(16 * which + core * SLOT, SLOT), :]
         parts = []
         for _ in range(3):
             parts.append(rest.astype(jnp.bfloat16))
@@ -464,8 +498,8 @@
             pltpu.VMEM((3, CHUNKS, 1, LANES), f32),
             pltpu.VMEM((3, 8, ROWS), f32),
             pltpu.VMEM((3, CHUNKS, 1, LANES), f32),
-            pltpu.VMEM((3, CHUNKS, 1, LANES), f32),
-            pltpu.VMEM((DEVICES, 3, 1, LANES), f32),
+            pltpu.VMEM((LANES // 16, CHUNKS, 1, LANES), f32),
+            pltpu.VMEM((DEVICES, 1, LANES), f32),
             pltpu.VMEM((3, DEVICES, ROWS), bf),
             pltpu.VMEM((LANES, DEVICES), f32),
             dma((4,)),

time: 65.7 us -> 62.3 us (0.948)
  Pallas kernels: 64.3 us -> 60.9 us
    pallas_call x1, Pallas kernels: 64.3 us -> 60.9 us  [body(): pl.pallas_call(kernel, out_shape=jax.ShapeDtypeStruct((1, ROWS), f32), in...]
where the time goes in v5:
time: 62.3 us; the launch traced here: 62.2 us
  Pallas kernels  60.9 us (98%)
  local copies, waits for them, and re-layouts  1.28 us (2%)
    pallas_call x1, Pallas kernels, body(): pl.pallas_call(kernel, out_shape=jax.ShapeDtypeStruct((1, ROWS), f32), in...  60.9 us
    unnamed x1, local copies, waits for them, and re-layouts  1.28 us

profile of v5, /device:TPU:1, one launch (start us, length us, event | category | flops | bytes accessed | tf_op | source)
XLA Modules:
  0.0 62.2 jit_solution(10007878054726768897)
XLA Ops:
  0.0 60.9 %dedup_scores.1 = f32[1,1024]{1,0:T(1,128)} custom-call(bf16[1024,1024]{1,0:T(8,128)(2,1)} %emb.1, s32[1,1024]{1,0:T(1,128)} %bitcast.5, s32[16,1,1024]{2,1,0:T(1,128)} %bitcast.3), custom_call_target="tpu_custom_call" | custom-call | tf_op jit(solution)/shard_map/dedup_scores/pallas_call | solution.py:482
  60.9 1.3 %copy.5 = f32[1024]{0:T(1024)} copy(f32[1024]{0:T(1024)} %bitcast.4) | data formatting | bytes 8192

commit v6 on v5

--- a/solution.py
+++ b/solution.py
@@ -42,7 +42,7 @@
     emb, tgt_hbm, lab, out,
     raw, unit, outgoing, recv, blk, tgt, lab_loc, lab_out, lab_in, lane_lab, col_lab, col_best, row_best, score, back, picks, turned,
     raw_sem, lab_sem, tgt_sem, self_sem, lab_ss, lab_rs, a2a_ss, a2a_rs, rl_ss, rl_rs, sib_ss, sib_rs,
-    back_ss, back_rs, row_sem,
+    back_ss, back_rs, plane_sem,
 ):
     gme = lax.axis_index("group")
     bme = lax.axis_index("block")
@@ -73,12 +73,18 @@
 
     barrier = pltpu.get_barrier_semaphore()
 
-    row = [lax.rem(bme + i, BLOCKS) for i in range(1, BLOCKS)]
-    column = [lax.rem(gme + i, GROUPS) for i in range(1, GROUPS)]
-    for block in row:
-        pl.semaphore_signal(barrier, inc=1, device_id=(gme, block), device_id_type=MESH)
-    for group in column:
+    images = [2 * lax.rem(xme + dx, 4) + core for dx in (2, 1, 3)]
+
+    def greet(i, _):
+        block = lax.rem(bme + i, BLOCKS)
+        for group in (gme, gsib):
+            pl.semaphore_signal(barrier, inc=1, device_id=(group, block), device_id_type=MESH)
+        return 0
+
+    lax.fori_loop(1, BLOCKS, greet, 0, unroll=False)
+    for group in images:
         pl.semaphore_signal(barrier, inc=1, device_id=(group, bme), device_id_type=MESH)
+    pl.semaphore_signal(barrier, inc=1, device_id=dev_sib, device_id_type=MESH)
 
     for which in range(3):
         col_best[which] = jnp.full((8, ROWS), LOW, jnp.float32)
@@ -132,82 +138,74 @@
                 second = (on_y & far_y) | (on_z & far_z)
                 block = z * 4 + y
                 other = jnp.where(on_y, block + way, block + 4 * along)
-                routes.append((c, dz, dy, block, jnp.where(second, NEAR, OWN), jnp.where(second, other, block)))
+                target = jnp.where(second, other, block)
+                hop = (on_y & (lax.rem(target, 4) != yme)) | (on_z & (target // 4 != zme))
+                which = jnp.where(second, NEAR, OWN)
+                routes.append((c, dz, dy, block, (which, jnp.where(hop, 1, 0)), target))
 
     def send(q, c, x, home_block, which, block):
         to_core = core if c == 0 else 1 - core
         pltpu.make_async_remote_copy(
             outgoing.at[lax.rem(class_me + q, 4) * 32 + home_block * 2 + to_core],
-            recv.at[which, class_me, zme, yme, core],
+            recv.at[which[0], class_me, zme, yme, core],
             a2a_ss,
-            a2a_rs.at[which, 2 * q + c],
+            a2a_rs.at[which[0], 2 * q + c, which[1]],
             device_id=(2 * x + to_core, block),
             device_id_type=MESH,
         ).start()
 
     def send_known(q):
         for c, dz, dy, home_block, which, block in routes:
-            dx = (q - dz - dy) % 4
-            if dz == 0 and dy == 0:
-                if dx or c:
-                    send(q, c, lax.rem(xme + dx, 4), home_block, which, block)
-            elif c == 0 and dx == 0:
-
-                @pl.when(block != bme)
-                def _():
-                    send(q, c, xme, home_block, which, block)
-
-    def send_rest(q, _):
-        for c, dz, dy, home_block, which, block in routes:
-            if dz == 0 and dy == 0:
+            if (dz + dy) % 4 != q:
                 continue
-            dx = lax.rem(q + 8 - dz - dy, 4)
 
             def go():
-                send(q, c, lax.rem(xme + dx, 4), home_block, which, block)
+                send(q, c, xme, home_block, which, block)
 
             if c == 0:
-                pl.when(dx != 0)(go)
+                pl.when(block != bme)(go)
             else:
                 go()
-        return 0
-
-    def send_all(q, _):
-        permute(q)
+
+    def send_rest(q, dxs):
         for c, dz, dy, home_block, which, block in routes:
-            dx = lax.rem(q + 8 - dz - dy, 4)
-
-            def go():
+            dx = (q - dz - dy) % 4
+            if dx:
                 send(q, c, lax.rem(xme + dx, 4), home_block, which, block)
 
-            if c == 0 and (dz or dy):
-                pl.when((dx != 0) | (block != bme))(go)
-            else:
-                go()
-        return 0
+    def here(dx):
+        pl.semaphore_wait(plane_sem.at[dx - 1], 1)
 
     permute(0)
-    pl.semaphore_wait(barrier, len(row) + len(column))
-    for block in row:
-        pl.semaphore_signal(row_sem, inc=1, device_id=(gme, block), device_id_type=MESH)
-    send_known(0)
+    pl.semaphore_wait(barrier, 2 * BLOCKS - 1 + len(images))
+    for dx, group in zip((2, 1, 3), images):
+        pl.semaphore_signal(plane_sem.at[3 - dx], inc=1, device_id=(group, bme), device_id_type=MESH)
+    for q in range(2):
+        if q:
+            permute(q)
+        send_known(q)
     pltpu.make_async_copy(
         outgoing.at[class_me * 32 + bme * 2 + core],
         recv.at[OWN, class_me, zme, yme, core],
-        a2a_rs.at[OWN, 0],
+        a2a_rs.at[OWN, 0, 0],
     ).start()
-    permute(1)
-    send_known(1)
-    pl.semaphore_wait(row_sem, len(row))
-    lax.fori_loop(0, 2, send_rest, 0, unroll=False)
-    lax.fori_loop(2, STAGES, send_all, 0, unroll=False)
+
+    for dx in (1, 3, 2):
+        here(dx)
+    send_rest(0, ())
+    send_rest(1, ())
+    for q in range(2, STAGES):
+        permute(q)
+        send_known(q)
+    send_rest(2, ())
+    send_rest(3, ())
 
     @pl.when(has_from)
     def _():
         pltpu.make_async_copy(
             outgoing.at[lax.rem(sum_from, 4) * 32 + from_block * 2 + core],
             recv.at[NEAR, class_me, zme, yme, core],
-            a2a_rs.at[NEAR, 2 * lax.rem(sum_from - sum_me + 4, 4)],
+            a2a_rs.at[NEAR, 2 * lax.rem(sum_from - sum_me + 4, 4), 0],
         ).start()
 
     for copy in lab_copies:
@@ -254,6 +252,7 @@
         for t in range(CHUNKS):
             lane_lab[which, t] = sides[which][:, t * LANES : (t + 1) * LANES]
 
+    four = recv.at[OWN, 0, 0, pl.ds(0, 2)]
     eight = recv.at[OWN, 0, 0]
     sixteen = recv.at[OWN, 0, pl.ds(0, 2)]
     thirty_two = recv.at[OWN, 0]
@@ -261,8 +260,9 @@
     def await_bytes(ref, sem):
         pltpu.make_async_copy(ref, ref, sem).wait()
 
-    def hand_on(which, n, a, c, dy, dz, block):
-        for step in range(2):
+    def hand_on(which, n, a, c, dy, dz, block, steps):
+        for step in steps:
+            await_bytes(four, a2a_rs.at[which, n, step])
             yy = lax.rem(yme + step * dy + 4, 4)
             zz = lax.rem(zme + step * dz + 4, 4)
 
@@ -289,19 +289,21 @@
         n = 2 * q + c
         from_core = lax.rem(core + c, 2)
 
-        @pl.when(has_to)
-        def _():
-            await_bytes(eight, a2a_rs.at[OWN, n])
-            hand_on(OWN, n, own_class(q), from_core, yme - to_block % 4, zme - to_block // 4, to_block)
+        for step in range(2):
+
+            @pl.when(has_to)
+            def _():
+                hand_on(OWN, n, own_class(q), from_core, yme - to_block % 4, zme - to_block // 4, to_block, (step,))
+
+            @pl.when(has_from)
+            def _():
+                hand_on(
+                    NEAR, n, near_class(q), from_core, yme - from_block % 4, zme - from_block // 4, from_block, (step,)
+                )
 
         @pl.when(jnp.logical_not(has_to))
         def _():
-            await_bytes(sixteen, a2a_rs.at[OWN, n])
-
-        @pl.when(has_from)
-        def _():
-            await_bytes(eight, a2a_rs.at[NEAR, n])
-            hand_on(NEAR, n, near_class(q), from_core, yme - from_block % 4, zme - from_block // 4, from_block)
+            await_bytes(sixteen, a2a_rs.at[OWN, n, 0])
 
     def lay_out(which, x):
         got = recv[which, x].astype(jnp.float32)
@@ -507,11 +509,11 @@
             dma,
             dma,
             dma, dma,
-            dma, dma((2, GROUPS)),
+            dma, dma((2, GROUPS, 2)),
             dma((2,)), dma((2, GROUPS)),
             dma, dma((STAGES,)),
             dma, dma,
-            pltpu.SemaphoreType.REGULAR,
+            pltpu.SemaphoreType.REGULAR((3,)),
         ],
         compiler_params=pltpu.CompilerParams(
             collective_id=0, has_side_effects=True, vmem_limit_bytes=60 * 2**20

time: 62.3 us -> 60.5 us (0.971)
  Pallas kernels: 60.9 us -> 59.1 us
    pallas_call x1, Pallas kernels: 60.9 us -> 59.1 us  [body(): pl.pallas_call(kernel, out_shape=jax.ShapeDtypeStruct((1, ROWS), f32), in...]
where the time goes in v6:
time: 60.5 us; the launch traced here: 60.4 us
  Pallas kernels  59.1 us (98%)
  local copies, waits for them, and re-layouts  1.28 us (2%)
    pallas_call x1, Pallas kernels, body(): pl.pallas_call(kernel, out_shape=jax.ShapeDtypeStruct((1, ROWS), f32), in...  59.1 us
    unnamed x1, local copies, waits for them, and re-layouts  1.28 us

profile of v6, /device:TPU:1, one launch (start us, length us, event | category | flops | bytes accessed | tf_op | source)
XLA Modules:
  0.0 60.4 jit_solution(868685714441887045)
XLA Ops:
  0.0 59.1 %dedup_scores.1 = f32[1,1024]{1,0:T(1,128)} custom-call(bf16[1024,1024]{1,0:T(8,128)(2,1)} %emb.1, s32[1,1024]{1,0:T(1,128)} %bitcast.5, s32[16,1,1024]{2,1,0:T(1,128)} %bitcast.3), custom_call_target="tpu_custom_call" | custom-call | tf_op jit(solution)/shard_map/dedup_scores/pallas_call | solution.py:484
  59.1 1.3 %copy.5 = f32[1024]{0:T(1024)} copy(f32[1024]{0:T(1024)} %bitcast.4) | data formatting | bytes 8192

commit v7 on v6

--- a/solution.py
+++ b/solution.py
@@ -415,30 +415,25 @@
     )
     own_back.start()
 
-    near_coords = [(lax.rem(zme + dz, 4), lax.rem(yme + dy, 4)) for dz in OFFSETS for dy in OFFSETS]
-
-    def give(i, _):
-        group = lax.rem(gme + 4 + i, GROUPS)
-        for n, (z, y) in enumerate(near_coords):
-            chunk = 2 * lax.rem(group // 2 + z + y, 4) + z // 2
-
-            def send():
-                pltpu.make_async_remote_copy(
-                    score.at[lax.rem(z, 2) * 4 + y, chunk],
-                    back.at[me],
-                    back_ss,
-                    back_rs,
-                    device_id=(group, z * 4 + y),
-                    device_id_type=MESH,
-                ).start()
-
-            if n == BLOCKS - 1:
-                pl.when(i != 4)(send)
-            else:
-                send()
-        return 0
-
-    lax.fori_loop(0, GROUPS, give, 0, unroll=False)
+    order = sorted(
+        ((dx, c, dz, dy) for dx in range(4) for c in range(2) for dz in range(4) for dy in range(4)),
+        key=lambda o: -sum(min(d, 4 - d) for d in (o[0], o[2], o[3])),
+    )
+    zs = [lax.rem(zme + d, 4) for d in range(4)]
+    ys = [lax.rem(yme + d, 4) for d in range(4)]
+    gs = [[2 * lax.rem(xme + d, 4) + c for c in (core, 1 - core)] for d in range(4)]
+    rows_at = [lax.rem(z, 2) * 4 for z in zs]
+    for dx, c, dz, dy in order:
+        if dx or c or dz or dy:
+            z, y = zs[dz], ys[dy]
+            pltpu.make_async_remote_copy(
+                score.at[rows_at[dz] + y, 2 * lax.rem(sum_me + dx + dz + dy, 4) + z // 2],
+                back.at[me],
+                back_ss,
+                back_rs,
+                device_id=(gs[dx][c], z * 4 + y),
+                device_id_type=MESH,
+            ).start()
 
     await_bytes(outgoing.at[pl.ds(0, DEVICES - 2)], a2a_ss)
 

time: 60.5 us -> 60.2 us (level)
  no operation moved by 1% of the time
where the time goes in v7:
time: 60.2 us; the launch traced here: 60.1 us
  Pallas kernels  58.8 us (98%)
  local copies, waits for them, and re-layouts  1.28 us (2%)
    pallas_call x1, Pallas kernels, body(): pl.pallas_call(kernel, out_shape=jax.ShapeDtypeStruct((1, ROWS), f32), in...  58.8 us
    unnamed x1, local copies, waits for them, and re-layouts  1.28 us

profile of v7, /device:TPU:1, one launch (start us, length us, event | category | flops | bytes accessed | tf_op | source)
XLA Modules:
  0.0 60.1 jit_solution(11464495503979192720)
XLA Ops:
  0.0 58.8 %dedup_scores.1 = f32[1,1024]{1,0:T(1,128)} custom-call(bf16[1024,1024]{1,0:T(8,128)(2,1)} %emb.1, s32[1,1024]{1,0:T(1,128)} %bitcast.5, s32[16,1,1024]{2,1,0:T(1,128)} %bitcast.3), custom_call_target="tpu_custom_call" | custom-call | tf_op jit(solution)/shard_map/dedup_scores/pallas_call | solution.py:479
  58.8 1.3 %copy.5 = f32[1024]{0:T(1024)} copy(f32[1024]{0:T(1024)} %bitcast.4) | data formatting | bytes 8192

commit v8 on v7

--- a/solution.py
+++ b/solution.py
@@ -68,23 +68,26 @@
     for i in range(4):
         b = jnp.clip(2 * place - 1 + i, 0, BLOCKS - 1)
         lab_copies.append(pltpu.make_async_copy(lab.at[b], lab_loc.at[i], lab_sem.at[i]))
-    for copy in raw_copies + [tgt_copy] + lab_copies:
+    for copy in raw_copies:
         copy.start()
 
     barrier = pltpu.get_barrier_semaphore()
 
     images = [2 * lax.rem(xme + dx, 4) + core for dx in (2, 1, 3)]
 
-    def greet(i, _):
-        block = lax.rem(bme + i, BLOCKS)
-        for group in (gme, gsib):
-            pl.semaphore_signal(barrier, inc=1, device_id=(group, block), device_id_type=MESH)
-        return 0
-
-    lax.fori_loop(1, BLOCKS, greet, 0, unroll=False)
-    for group in images:
-        pl.semaphore_signal(barrier, inc=1, device_id=(group, bme), device_id_type=MESH)
-    pl.semaphore_signal(barrier, inc=1, device_id=dev_sib, device_id_type=MESH)
+    offsets = sorted(
+        ((dz, dy) for dz in range(4) for dy in range(4)), key=lambda o: -min(o[0], 4 - o[0]) - min(o[1], 4 - o[1])
+    )
+    peers = [
+        (group, lax.rem(zme + dz, 4) * 4 + lax.rem(yme + dy, 4))
+        for dz, dy in offsets
+        for group in (gme, gsib)
+    ][:-2]
+    peers = peers[:10] + [(group, bme) for group in images] + peers[10:] + [dev_sib]
+    for peer in peers:
+        pl.semaphore_signal(barrier, inc=1, device_id=peer, device_id_type=MESH)
+    for copy in [tgt_copy] + lab_copies:
+        copy.start()
 
     for which in range(3):
         col_best[which] = jnp.full((8, ROWS), LOW, jnp.float32)

time: 60.2 us -> 60.2 us (level)
  no operation moved by 1% of the time
where the time goes in v8:
time: 60.2 us; the launch traced here: 60 us
  Pallas kernels  58.7 us (98%)
  local copies, waits for them, and re-layouts  1.28 us (2%)
    pallas_call x1, Pallas kernels, body(): pl.pallas_call(kernel, out_shape=jax.ShapeDtypeStruct((1, ROWS), f32), in...  58.7 us
    unnamed x1, local copies, waits for them, and re-layouts  1.28 us

profile of v8, /device:TPU:1, one launch (start us, length us, event | category | flops | bytes accessed | tf_op | source)
XLA Modules:
  0.0 60.0 jit_solution(14315952327314288504)
XLA Ops:
  0.0 58.7 %dedup_scores.1 = f32[1,1024]{1,0:T(1,128)} custom-call(bf16[1024,1024]{1,0:T(8,128)(2,1)} %emb.1, s32[1,1024]{1,0:T(1,128)} %bitcast.5, s32[16,1,1024]{2,1,0:T(1,128)} %bitcast.3), custom_call_target="tpu_custom_call" | custom-call | tf_op jit(solution)/shard_map/dedup_scores/pallas_call | solution.py:482
  58.7 1.3 %copy.5 = f32[1024]{0:T(1024)} copy(f32[1024]{0:T(1024)} %bitcast.4) | data formatting | bytes 8192
